TPU v7x, 32 devices: a whole 2x2x4 slice. The times are simulated.
32 devices in a mesh: tm: 8 (over y, x, core), cell: 4 (over z).
Axes of the slice: x: 2, y: 2, z: 4, core: 2. Of those that a mesh axis runs over, the one named last changes fastest.
Arguments:
- start_states: float32 [8, 3, 128, 512], P('tm', None, None, 'cell'), may hold values from -6 to 6
- ocean_mask: int32 [128, 512], P(None, 'cell'), may hold values 0 or 1
- depth_class: int32 [128, 512], P(None, 'cell'), may hold values from 0 to 7
- class_depth: float32 [8], replicated, may hold values from 0.2 to 1
- drag_rate: float32 [128, 512], P(None, 'cell'), may hold values from 0.02 to 0.3
- tide_cos: float32 [128, 512], P(None, 'cell'), may hold values from -3 to 3
- tide_sin: float32 [128, 512], P(None, 'cell'), may hold values from -3 to 3
Outputs:
- defect: float32 [8, 3, 128, 512], P('tm', None, None, 'cell')
- state_grad: float32 [8, 3, 128, 512], P('tm', None, None, 'cell')
- drag_grad: float32 [128, 512], P('tm', 'cell')
All inputs are finite; a program needn't handle non-finite values. No bound on the sum of `ocean_mask` on one device may be relied on, other than what follows from the above.
Results may differ from a plain program's by a relative error of at most 0.00002.
Values sent between devices are 32-bit elements; how exact they have to be, the bound alone decides.
A program may use at most 64 MiB of HBM per device.

v0:
```python
import math

import jax
import jax.numpy as jnp
from jax import lax
from jax.sharding import PartitionSpec as P

STEPS = 8


FLUX_RATE = 0.7
PRESS_RATE = 0.7
ROTATION_RATE = 0.15


def with_halo(block, sides, width):
    for axis, dim in sides:
        count = lax.axis_size(axis)
        forward = [(i, i + 1) for i in range(count - 1)]
        forward.append((count - 1, 0))
        backward = [(target, source) for source, target in forward]
        low = lax.ppermute(
            lax.slice_in_dim(block, block.shape[dim] - width, None, axis=dim), axis, forward
        )
        high = lax.ppermute(lax.slice_in_dim(block, 0, width, axis=dim), axis, backward)
        block = jnp.concatenate([low, block, high], axis=dim)
    return block


def from_behind(value, axis, steps):
    count = lax.axis_size(axis)
    pairs = [(source, (source + steps) % count) for source in range(count)]
    return lax.ppermute(value, axis, pairs)


def cropped(values_in, cut_width):
    if cut_width == 0:
        return values_in
    return values_in[..., cut_width : values_in.shape[-1] - cut_width]


def across_cols(values_in):
    return 0.5 * (values_in[..., 2:] - values_in[..., :-2])


def across_rows(values_in):
    zeros_row = jnp.zeros_like(values_in[..., :1, :])
    upper_rows = jnp.concatenate([values_in[..., 1:, :], zeros_row], axis=-2)
    lower_rows = jnp.concatenate([zeros_row, values_in[..., :-1, :]], axis=-2)
    return 0.5 * (upper_rows - lower_rows)


def coriolis(rows_count):
    latitude = math.pi * ((jnp.arange(rows_count, dtype=jnp.float32) + 0.5) / rows_count - 0.5)
    return (ROTATION_RATE * jnp.sin(latitude))[:, None]


def advance_wide(current, statics, rotation, cosine, sine_now):
    sea_mask, depth_field, retain = (statics[0], statics[1], statics[2])
    height, east_vel, north_vel = (current[0], current[1], current[2])
    spread = across_cols(depth_field * east_vel) + cropped(across_rows(depth_field * north_vel), 1)
    height_new = cropped(sea_mask, 1) * (cropped(height, 1) - FLUX_RATE * spread)
    surface = height_new + cropped(cosine * statics[3] + sine_now * statics[4], 1)
    mask_keep = cropped(sea_mask * retain, 2)
    east_mid = cropped(east_vel, 2)
    north_mid = cropped(north_vel, 2)
    east_new = mask_keep * (east_mid - PRESS_RATE * across_cols(surface) + rotation * north_mid)
    north_new = mask_keep * (
        north_mid - PRESS_RATE * cropped(across_rows(surface), 1) - rotation * east_mid
    )
    return jnp.stack([cropped(height_new, 1), east_new, north_new])


def adjoint_step(adjoint, statics, rotation):
    sea_mask, depth_field, retain = (statics[0], statics[1], statics[2])
    mask_keep = sea_mask * retain
    east_part = mask_keep * adjoint[1]
    north_part = mask_keep * adjoint[2]
    summed = cropped(adjoint[0], 1) + PRESS_RATE * (
        across_cols(east_part) + cropped(across_rows(north_part), 1)
    )
    height_part = cropped(sea_mask, 1) * summed
    depth_flux = FLUX_RATE * cropped(depth_field, 2)
    east_in = (
        cropped(east_part, 2)
        - rotation * cropped(north_part, 2)
        + depth_flux * across_cols(height_part)
    )
    north_in = (
        cropped(north_part, 2)
        + rotation * cropped(east_part, 2)
        + depth_flux * cropped(across_rows(height_part), 1)
    )
    return (jnp.stack([cropped(height_part, 1), east_in, north_in]), east_part, north_part)


def local(start_states, ocean_mask, depth_class, class_depth, drag_rate, tide_cos, tide_sin):
    per_rim = STEPS
    rim_width = 2 * per_rim
    slice_count = lax.axis_size("tm")
    slice_index = lax.axis_index("tm")
    sea_mask = ocean_mask.astype(jnp.float32)
    classes = jnp.arange(class_depth.shape[0], dtype=jnp.int32)
    depth_field = jnp.sum(
        jnp.where(depth_class[None] == classes[:, None, None], class_depth[:, None, None], 0.0),
        axis=0,
    )
    retain = 1.0 / (1.0 + drag_rate)
    statics = with_halo(
        jnp.stack([sea_mask, depth_field, retain, tide_cos, tide_sin]), (("cell", 2),), rim_width
    )
    rotation = coriolis(sea_mask.shape[0])
    initial = start_states[0]
    current = initial * sea_mask
    phase_unit = 2.0 * math.pi / (slice_count * STEPS)
    stored = []
    first_step = 0
    widened = with_halo(current, (("cell", 2),), rim_width)
    for inner_step in range(per_rim):
        phase_now = (slice_index * STEPS + first_step + inner_step).astype(jnp.float32) * phase_unit
        widened = advance_wide(
            widened,
            cropped(statics, 2 * inner_step),
            rotation,
            jnp.cos(phase_now),
            jnp.sin(phase_now),
        )
        stored.append(cropped(widened[1:], rim_width - 2 * inner_step - 2))
    current = widened
    arrived = from_behind(current, "tm", 1)
    behind = sea_mask * (arrived - initial)
    defect = from_behind(behind, "tm", -1)
    drag_total = jnp.zeros_like(drag_rate)
    first_step = 0
    widened = with_halo(defect, (("cell", 2),), rim_width)
    for inner_step in range(per_rim):
        step_number = first_step + per_rim - 1 - inner_step
        margin = rim_width - 2 * inner_step
        widened, east_part, north_part = adjoint_step(
            widened, cropped(statics, 2 * inner_step), rotation
        )
        outputs = stored[step_number]
        drag_total = drag_total - (
            cropped(east_part, margin) * outputs[0] + cropped(north_part, margin) * outputs[1]
        )
    state_grad = sea_mask * widened - behind
    summed_rows = lax.psum_scatter(drag_total, "tm", scatter_dimension=0, tiled=True)
    drag_grad = summed_rows / slice_count
    return (defect[None], state_grad[None], drag_grad)


def solution(mesh):
    return jax.shard_map(
        local,
        mesh=mesh,
        in_specs=(
            P("tm", None, None, "cell"),
            P(None, "cell"),
            P(None, "cell"),
            P(),
            P(None, "cell"),
            P(None, "cell"),
            P(None, "cell"),
        ),
        out_specs=(P("tm", None, None, "cell"), P("tm", None, None, "cell"), P("tm", "cell")),
        check_vma=False,
    )
```

profile of v0, /device:TPU:0, one launch (start us, length us, event | category | flops | bytes accessed | tf_op | source)
XLA Modules:
  0.0 115.5 jit_solution(10657184798336107065)
XLA Ops:
  7.2 0.8 bitcast_dynamic-update-slice_fusion.4
  8.2 0.8 copy-done.3
  9.1 0.8 copy-done.4
  9.9 0.8 copy-done.5
  10.9 3.1 %collective-permute-start = (f32[5,128,16]{2,1,0:T(8,128)S(1)}, f32[5,128,16]{2,1,0:T(8,128)S(1)}, u32[]{:S(2)}, u32[]{:S(2)}) collective-permute-start(f32[5,128,16]{2,1,0:T(8,128)S(1)} %get-tuple-element.118), channel_id=1, source_target_pairs={{0,1},{1,2},{2,3},{3,0},{4,5},{5,6},{6,7},{7,4},{8,9},{9,10},{10,1... | collective-permute-start | bytes 122888 | tf_op jit(solution)/shard_map/ppermute | solution.py:22
  14.0 2.1 %collective-permute-start.1 = (f32[5,128,16]{2,1,0:T(8,128)S(1)}, f32[5,128,16]{2,1,0:T(8,128)S(1)}, u32[]{:S(2)}, u32[]{:S(2)}) collective-permute-start(f32[5,128,16]{2,1,0:T(8,128)S(1)} %get-tuple-element.119), channel_id=1, source_target_pairs={{1,0},{2,1},{3,2},{0,3},{5,4},{6,5},{7,6},{4,7},{9,8},{10,9},{11,1... | collective-permute-start | bytes 122888 | tf_op jit(solution)/shard_map/ppermute | solution.py:25
  16.3 3.8 %collective-permute-start.3 = (f32[3,128,16]{2,1,0:T(8,128)S(1)}, f32[3,128,16]{2,1,0:T(8,128)S(1)}, u32[]{:S(2)}, u32[]{:S(2)}) collective-permute-start(f32[3,128,16]{2,1,0:T(8,128)S(1)} %get-tuple-element.123), channel_id=1, source_target_pairs={{1,0},{2,1},{3,2},{0,3},{5,4},{6,5},{7,6},{4,7},{9,8},{10,9},{11,1... | collective-permute-start | bytes 73736 | tf_op jit(solution)/shard_map/ppermute | solution.py:25
  21.4 14.5 %collective-permute-done.2 = f32[3,128,16]{2,1,0:T(8,128)S(1)} collective-permute-done((f32[3,128,16]{2,1,0:T(8,128)S(1)}, f32[3,128,16]{2,1,0:T(8,128)S(1)}, u32[]{:S(2)}, u32[]{:S(2)}) %collective-permute-start.2) | collective-permute-done | bytes 24608 | tf_op jit(solution)/shard_map/ppermute | solution.py:22
  35.9 2.7 %collective-permute-done.3 = f32[3,128,16]{2,1,0:T(8,128)S(1)} collective-permute-done((f32[3,128,16]{2,1,0:T(8,128)S(1)}, f32[3,128,16]{2,1,0:T(8,128)S(1)}, u32[]{:S(2)}, u32[]{:S(2)}) %collective-permute-start.3) | collective-permute-done | bytes 24608 | tf_op jit(solution)/shard_map/ppermute | solution.py:25
  40.6 0.4 fusion.295
  41.5 0.4 fusion.298
  42.4 0.4 fusion.299
  43.4 0.4 fusion.302
  46.6 6.0 %collective-permute-done.4 = f32[3,128,128]{2,1,0:T(8,128)S(1)} collective-permute-done((f32[3,128,128]{2,1,0:T(8,128)S(1)}, f32[3,128,128]{2,1,0:T(8,128)S(1)}, u32[]{:S(2)}, u32[]{:S(2)}) %collective-permute-start.4) | collective-permute-done | bytes 196640 | tf_op jit(solution)/shard_map/ppermute | solution.py:33
  52.6 3.2 %collective-permute-done.5 = f32[3,128,128]{2,1,0:T(8,128)S(1)} collective-permute-done((f32[3,128,128]{2,1,0:T(8,128)S(1)}, f32[3,128,128]{2,1,0:T(8,128)S(1)}, u32[]{:S(2)}, u32[]{:S(2)}) %collective-permute-start.5) | collective-permute-done | bytes 196640 | tf_op jit(solution)/shard_map/ppermute | solution.py:33
  55.9 1.2 %collective-permute-start.6 = (f32[3,128,16]{2,1,0:T(8,128)S(1)}, f32[3,128,16]{2,1,0:T(8,128)S(1)}, u32[]{:S(2)}, u32[]{:S(2)}) collective-permute-start(f32[3,128,16]{2,1,0:T(8,128)S(1)} %get-tuple-element.120), channel_id=1, source_target_pairs={{0,1},{1,2},{2,3},{3,0},{4,5},{5,6},{6,7},{7,4},{8,9},{9,10},{10,1... | collective-permute-start | bytes 73736 | tf_op jit(solution)/shard_map/ppermute | solution.py:22
  57.1 2.7 %collective-permute-start.7 = (f32[3,128,16]{2,1,0:T(8,128)S(1)}, f32[3,128,16]{2,1,0:T(8,128)S(1)}, u32[]{:S(2)}, u32[]{:S(2)}) collective-permute-start(f32[3,128,16]{2,1,0:T(8,128)S(1)} %get-tuple-element.121), channel_id=1, source_target_pairs={{1,0},{2,1},{3,2},{0,3},{5,4},{6,5},{7,6},{4,7},{9,8},{10,9},{11,1... | collective-permute-start | bytes 73736 | tf_op jit(solution)/shard_map/ppermute | solution.py:25
  59.8 5.8 %collective-permute-done.6 = f32[3,128,16]{2,1,0:T(8,128)S(1)} collective-permute-done((f32[3,128,16]{2,1,0:T(8,128)S(1)}, f32[3,128,16]{2,1,0:T(8,128)S(1)}, u32[]{:S(2)}, u32[]{:S(2)}) %collective-permute-start.6) | collective-permute-done | bytes 24608 | tf_op jit(solution)/shard_map/ppermute | solution.py:22
  65.6 3.1 %collective-permute-done.7 = f32[3,128,16]{2,1,0:T(8,128)S(1)} collective-permute-done((f32[3,128,16]{2,1,0:T(8,128)S(1)}, f32[3,128,16]{2,1,0:T(8,128)S(1)}, u32[]{:S(2)}, u32[]{:S(2)}) %collective-permute-start.7) | collective-permute-done | bytes 24608 | tf_op jit(solution)/shard_map/ppermute | solution.py:25
  73.2 1.3 %fusion.246 = f32[128,128]{1,0:T(8,128)} fusion(f32[1,128,156]{2,1,0:T(8,128)S(1)} %bitcast.302, f32[1,128,156]{2,1,0:T(8,128)S(1)} %bitcast.301, f32[1,128,152]{2,1,0:T(8,128)S(1)} %bitcast.303, f32[128,136]{1,0:T(8,128)S(1)} %get-tuple-element.98, f32[1,128,152]{2,1,0:T(8,128)S(1)} %bitcast.304, f32[128,136]{1,0:T(8,128)S(1)} %get-tuple-element.97, ...), kind=kLoop, calls=%fused_computation.377 | loop fusion | flops 524288 | bytes 2162688 | tf_op jit(solution)/shard_map/sub | solution.py:143
  75.0 0.7 fusion.1
  75.7 31.0 %reduce-scatter.2.cloned.1.call-done = f32[16,128]{1,0:T(8,128)} async-done(((f32[128,128]{1,0:T(8,128)}), f32[16,128]{1,0:T(8,128)}) %reduce-scatter.2.cloned.1.call-update) | async-done | bytes 8208 | tf_op jit(solution)/shard_map/reduce_scatter | solution.py:147
  106.7 1.3 %broadcast_multiply_fusion = f32[16,128]{1,0:T(8,128)} fusion(f32[16,128]{1,0:T(8,128)} %reduce-scatter.2.cloned.1.call-done), kind=kLoop, calls=%fused_computation.449 | loop fusion | flops 2048 | bytes 16384 | tf_op jit(solution)/shard_map/div | solution.py:148
  108.0 0.7 copy.15
  (107 shorter events, 11.7 us)
Async XLA Ops:
  7.2 0.9 copy-start.6
  7.2 0.9 copy-start.2
  7.2 99.5 %reduce-scatter.2.cloned.1.call-start = ((), (), s32[]{:S(2)}) async-start(), calls=%async_computation.1 | async-start | bytes 73728 | tf_op jit(solution)/shard_map/reduce_scatter | solution.py:147
  8.2 0.8 copy-start.3
  9.1 0.8 copy-start.4
  9.9 0.8 copy-start.5
  10.7 5.3 %copy-start.1 = (s32[128,128]{1,0:T(8,128)S(1)}, s32[128,128]{1,0:T(8,128)}, u32[]{:S(2)}) copy-start(s32[128,128]{1,0:T(8,128)} %param.8) | copy-start | bytes 196612
  10.7 5.4 %copy-start = (f32[1,3,128,128]{3,2,1,0:T(8,128)S(1)}, f32[1,3,128,128]{3,2,1,0:T(8,128)}, u32[]{:S(2)}) copy-start(f32[1,3,128,128]{3,2,1,0:T(8,128)} %param.7) | copy-start | bytes 589828
  10.9 28.0 %collective-permute-start = (f32[5,128,16]{2,1,0:T(8,128)S(1)}, f32[5,128,16]{2,1,0:T(8,128)S(1)}, u32[]{:S(2)}, u32[]{:S(2)}) collective-permute-start(f32[5,128,16]{2,1,0:T(8,128)S(1)} %get-tuple-element.118), channel_id=1, source_target_pairs={{0,1},{1,2},{2,3},{3,0},{4,5},{5,6},{6,7},{7,4},{8,9},{9,10},{10,1... | collective-permute-start | bytes 122888 | tf_op jit(solution)/shard_map/ppermute | solution.py:22
  14.0 24.9 %collective-permute-start.1 = (f32[5,128,16]{2,1,0:T(8,128)S(1)}, f32[5,128,16]{2,1,0:T(8,128)S(1)}, u32[]{:S(2)}, u32[]{:S(2)}) collective-permute-start(f32[5,128,16]{2,1,0:T(8,128)S(1)} %get-tuple-element.119), channel_id=1, source_target_pairs={{1,0},{2,1},{3,2},{0,3},{5,4},{6,5},{7,6},{4,7},{9,8},{10,9},{11,1... | collective-permute-start | bytes 122888 | tf_op jit(solution)/shard_map/ppermute | solution.py:25
  16.2 19.6 %collective-permute-start.2 = (f32[3,128,16]{2,1,0:T(8,128)S(1)}, f32[3,128,16]{2,1,0:T(8,128)S(1)}, u32[]{:S(2)}, u32[]{:S(2)}) collective-permute-start(f32[3,128,16]{2,1,0:T(8,128)S(1)} %get-tuple-element.122), channel_id=1, source_target_pairs={{0,1},{1,2},{2,3},{3,0},{4,5},{5,6},{6,7},{7,4},{8,9},{9,10},{10,1... | collective-permute-start | bytes 73736 | tf_op jit(solution)/shard_map/ppermute | solution.py:22
  16.3 22.3 %collective-permute-start.3 = (f32[3,128,16]{2,1,0:T(8,128)S(1)}, f32[3,128,16]{2,1,0:T(8,128)S(1)}, u32[]{:S(2)}, u32[]{:S(2)}) collective-permute-start(f32[3,128,16]{2,1,0:T(8,128)S(1)} %get-tuple-element.123), channel_id=1, source_target_pairs={{1,0},{2,1},{3,2},{0,3},{5,4},{6,5},{7,6},{4,7},{9,8},{10,9},{11,1... | collective-permute-start | bytes 73736 | tf_op jit(solution)/shard_map/ppermute | solution.py:25
  46.5 6.0 %collective-permute-start.4 = (f32[3,128,128]{2,1,0:T(8,128)S(1)}, f32[3,128,128]{2,1,0:T(8,128)S(1)}, u32[]{:S(2)}, u32[]{:S(2)}) collective-permute-start(f32[3,128,128]{2,1,0:T(8,128)S(1)} %pad_maximum_fusion.3), channel_id=1, source_target_pairs={{0,4},{4,8},{8,12},{12,16},{16,20},{20,24},{24,28},{28,0},{1,5},{5... | collective-permute-start | bytes 589832 | tf_op jit(solution)/shard_map/ppermute | solution.py:33
  52.6 3.2 %collective-permute-start.5 = (f32[3,128,128]{2,1,0:T(8,128)S(1)}, f32[3,128,128]{2,1,0:T(8,128)S(1)}, u32[]{:S(2)}, u32[]{:S(2)}) collective-permute-start(f32[3,128,128]{2,1,0:T(8,128)S(1)} %fusion.2), channel_id=1, source_target_pairs={{0,28},{4,0},{8,4},{12,8},{16,12},{20,16},{24,20},{28,24},{1,29},{... | collective-permute-start | bytes 589832 | tf_op jit(solution)/shard_map/ppermute | solution.py:33
  55.9 9.7 %collective-permute-start.6 = (f32[3,128,16]{2,1,0:T(8,128)S(1)}, f32[3,128,16]{2,1,0:T(8,128)S(1)}, u32[]{:S(2)}, u32[]{:S(2)}) collective-permute-start(f32[3,128,16]{2,1,0:T(8,128)S(1)} %get-tuple-element.120), channel_id=1, source_target_pairs={{0,1},{1,2},{2,3},{3,0},{4,5},{5,6},{6,7},{7,4},{8,9},{9,10},{10,1... | collective-permute-start | bytes 73736 | tf_op jit(solution)/shard_map/ppermute | solution.py:22
  57.1 11.6 %collective-permute-start.7 = (f32[3,128,16]{2,1,0:T(8,128)S(1)}, f32[3,128,16]{2,1,0:T(8,128)S(1)}, u32[]{:S(2)}, u32[]{:S(2)}) collective-permute-start(f32[3,128,16]{2,1,0:T(8,128)S(1)} %get-tuple-element.121), channel_id=1, source_target_pairs={{1,0},{2,1},{3,2},{0,3},{5,4},{6,5},{7,6},{4,7},{9,8},{10,9},{11,1... | collective-permute-start | bytes 73736 | tf_op jit(solution)/shard_map/ppermute | solution.py:25
Sparse Core Ops, SparseCore 0:
  74.7 32.0 reduce-scatter.1
where the time goes:
time: 116 us
  waiting for transfers between devices  66.3 us (57%)
  other arithmetic  16 us (14%)
  between operations  15.9 us (14%)
  starting transfers between devices  13.1 us (11%)
  local copies, waits for them, and re-layouts  4.3 us (4%)
    reduce_scatter x1, waiting for transfers between devices, local(): lax.psum_scatter(drag_total, 'tm', scatter_dimension=0, tiled=True)  31 us
    ppermute x3, waiting for transfers between devices, with_halo(): lax.ppermute(lax.slice_in_dim(block, block.shape[dim] - width, None, axis...  20.3 us
    ppermute x2, waiting for transfers between devices, from_behind(): return lax.ppermute(value, axis, pairs)  9.16 us
    ppermute x3, starting transfers between devices, with_halo(): lax.ppermute(lax.slice_in_dim(block, 0, width, axis=dim), axis, backward)  8.6 us
    ppermute x3, waiting for transfers between devices, with_halo(): lax.ppermute(lax.slice_in_dim(block, 0, width, axis=dim), axis, backward)  5.83 us
    ppermute x3, starting transfers between devices, with_halo(): lax.ppermute(lax.slice_in_dim(block, block.shape[dim] - width, None, axis...  4.32 us
    unnamed x17, local copies, waits for them, and re-layouts  3.18 us
  transfers between devices with their start and end apart: 9, of which 7 were waited for; matrix products, arithmetic and copies ran while one was open for 1% of the time, Pallas kernels for 0%

commit v1 on v0

v1 whole, which is shorter than its diff:
```python
import functools
import math

import jax
import jax.numpy as jnp
from jax import lax
from jax.experimental import pallas as pl
from jax.experimental.pallas import tpu as pltpu
from jax.sharding import PartitionSpec as P

STEPS = 8
FLUX_RATE = 0.7
PRESS_RATE = 0.7
ROTATION_RATE = 0.15

LANES = 128
RIM = 4 * STEPS
PAD = 8
BLOCK = 32
MESH = pl.DeviceIdType.MESH

SEA, KEEP, DEPTH, COS, SIN = range(5)


def kernel(
    slices,
    cells,
    start_ref,
    mask_ref,
    class_ref,
    table_ref,
    drag_ref,
    cos_ref,
    sin_ref,
    defect_out,
    grad_out,
    drag_out,
    start,
    mask,
    classes,
    drag,
    tides,
    statics,
    rotation,
    trig,
    height,
    east,
    north,
    east_rim,
    north_rim,
    flux,
    press,
    packed,
    arrived,
    next_rim,
    next_start,
    defect,
    behind,
    grad,
    total,
    shares,
    share_in,
    share_out,
    in_sem,
    out_sem,
    halo_send,
    halo_recv,
    next_send,
    next_recv,
    rim_send,
    rim_recv,
    behind_send,
    behind_recv,
    share_send,
    share_recv,
):
    rows = mask.shape[0]
    blocks = rows // BLOCK
    me = lax.axis_index("tm")
    cell = lax.axis_index("cell")
    ahead = lax.rem(me + 1, slices)
    back = lax.rem(me + slices - 1, slices)
    east_cell = lax.rem(cell + 1, cells)
    west_cell = lax.rem(cell + cells - 1, cells)

    barrier = pltpu.get_barrier_semaphore()
    for other in (west_cell, east_cell):
        pl.semaphore_signal(barrier, inc=1, device_id=(me, other), device_id_type=MESH)
    for step in range(1, slices):
        peer = lax.rem(me + step, slices)
        pl.semaphore_signal(barrier, inc=1, device_id=(peer, cell), device_id_type=MESH)

    loads = [
        pltpu.make_async_copy(source, target, in_sem.at[i])
        for i, (source, target) in enumerate(
            (
                (mask_ref, mask),
                (class_ref, classes),
                (drag_ref, drag),
                (cos_ref, tides.at[0]),
                (sin_ref, tides.at[1]),
                (start_ref.at[0], start),
            )
        )
    ]
    for load in loads:
        load.start()
    for load in loads:
        load.wait()

    lane = lax.broadcasted_iota(jnp.int32, (BLOCK, LANES), 1)
    first = lane == 0
    last = lane == LANES - 1
    slot = lane // RIM

    def span(b):
        return pl.ds(b * BLOCK, BLOCK)

    def across(body, rim):
        body_up = pltpu.roll(jnp.where(first, rim, body), LANES - 1, 1)
        body_down = pltpu.roll(jnp.where(last, rim, body), 1, 1)
        rim_up = pltpu.roll(jnp.where(first, body, rim), LANES - 1, 1)
        rim_down = pltpu.roll(jnp.where(last, body, rim), 1, 1)
        return (body_up - body_down, rim_up - rim_down)

    def across_body(body, rim):
        body_up = pltpu.roll(jnp.where(first, rim, body), LANES - 1, 1)
        body_down = pltpu.roll(jnp.where(last, rim, body), 1, 1)
        return body_up - body_down

    def along(ref, half, b):
        upper = ref[half, pl.ds(PAD + b * BLOCK + 1, BLOCK), :]
        lower = ref[half, pl.ds(PAD + b * BLOCK - 1, BLOCK), :]
        return upper - lower

    def inner(b):
        return pl.ds(PAD + b * BLOCK, BLOCK)

    def turned(value, by):
        return value if by == 0 else pltpu.roll(value, by * RIM, 1)

    def pack(parts):
        to_west = parts[0]
        to_east = parts[0]
        for f in range(1, 4):
            to_west = jnp.where(slot == f, parts[f], to_west)
            to_east = jnp.where(slot == (f + 3) % 4, parts[f], to_east)
        return to_west, to_east

    for b in range(blocks):
        at = span(b)
        sea = mask[at, :].astype(jnp.float32)
        depth = jnp.zeros((BLOCK, LANES), jnp.float32)
        kind = classes[at, :]
        for c in range(table_ref.shape[0]):
            depth = jnp.where(kind == c, table_ref[c], depth)
        depth = (0.5 * FLUX_RATE) * depth
        keep = sea / (1.0 + drag[at, :])
        cosine = (0.5 * PRESS_RATE) * tides[0, at, :]
        sine = (0.5 * PRESS_RATE) * tides[1, at, :]
        fields = (sea, keep, depth, cosine, sine)
        for f in range(5):
            statics[f, 0, at, :] = fields[f]
        west, east_side = pack([turned(fields[f + 1], f) for f in range(4)])
        packed[0, at, :] = west
        packed[1, at, :] = east_side
    for b in range(blocks - 1):
        parts = [turned(start[f, span(b), :], f) for f in range(3)]
        parts.append(turned(start[b, span(blocks - 1), :], 3))
        west, east_side = pack(parts)
        packed[0, pl.ds(rows + b * BLOCK, BLOCK), :] = west
        packed[1, pl.ds(rows + b * BLOCK, BLOCK), :] = east_side

    pl.semaphore_wait(barrier, slices + 1)

    halos = [
        pltpu.make_async_remote_copy(
            src_ref=packed.at[side],
            dst_ref=arrived.at[side],
            send_sem=halo_send.at[side],
            recv_sem=halo_recv.at[side],
            device_id=(me, other),
            device_id_type=MESH,
        )
        for side, other in ((0, west_cell), (1, east_cell))
    ]
    for halo in halos:
        halo.start()
    start_copy = pltpu.make_async_remote_copy(
        src_ref=start,
        dst_ref=next_start,
        send_sem=next_send,
        recv_sem=next_recv,
        device_id=(back, cell),
        device_id_type=MESH,
    )
    start_copy.start()

    latitude = lax.broadcasted_iota(jnp.int32, (rows, LANES), 0).astype(jnp.float32)
    latitude = math.pi * ((latitude + 0.5) / rows - 0.5)
    rotation[...] = ROTATION_RATE * jnp.sin(latitude)
    unit = 2.0 * math.pi / (slices * STEPS)
    number = lax.broadcasted_iota(jnp.int32, (STEPS, LANES), 0) + me * STEPS
    phase = number.astype(jnp.float32) * unit
    trig[0:STEPS, :] = jnp.cos(phase)
    trig[STEPS : 2 * STEPS, :] = jnp.sin(phase)
    blank = jnp.zeros((PAD, LANES), jnp.float32)
    for ref in (flux, press):
        for half in range(2):
            ref[half, 0:PAD, :] = blank
            ref[half, PAD + rows : 2 * PAD + rows, :] = blank
    for b in range(blocks):
        at = span(b)
        sea = statics[SEA, 0, at, :]
        height[0, at, :] = sea * start[0, at, :]
        east[0, at, :] = sea * start[1, at, :]
        north_now = sea * start[2, at, :]
        north[0, at, :] = north_now
        flux[0, inner(b), :] = statics[DEPTH, 0, at, :] * north_now

    for halo in halos:
        halo.wait_recv()
    relays = [
        pltpu.make_async_remote_copy(
            src_ref=arrived.at[side, pl.ds(rows, rows - BLOCK)],
            dst_ref=next_rim.at[side],
            send_sem=rim_send.at[side],
            recv_sem=rim_recv.at[side],
            device_id=(back, cell),
            device_id_type=MESH,
        )
        for side in range(2)
    ]
    for relay in relays:
        relay.start()

    def unpack(ref, at, f):
        both = jnp.where(
            slot == f, ref[0, at, :], jnp.where(slot == (f + 3) % 4, ref[1, at, :], 0.0)
        )
        return turned(both, (4 - f) % 4)

    def unpack_state(ref, offset, f, b):
        if b < blocks - 1:
            return unpack(ref, pl.ds(offset + b * BLOCK, BLOCK), f)
        return unpack(ref, pl.ds(offset + f * BLOCK, BLOCK), 3)

    for b in range(blocks):
        at = span(b)
        fields = [unpack(arrived, at, f) for f in range(4)]
        sea = jnp.where(fields[0] > 0.0, 1.0, 0.0)
        statics[SEA, 1, at, :] = sea
        for f in range(4):
            statics[f + 1, 1, at, :] = fields[f]
        state = [sea * unpack_state(arrived, rows, f, b) for f in range(3)]
        height[1, at, :] = state[0]
        east_rim[at, :] = state[1]
        north_rim[at, :] = state[2]
        flux[1, inner(b), :] = fields[1] * state[2]

    def forward(n, carry):
        cosine = trig[pl.ds(n, 1), :]
        sine = trig[pl.ds(STEPS + n, 1), :]
        for b in range(blocks):
            at = span(b)
            spread = across(
                statics[DEPTH, 0, at, :] * east[n, at, :],
                statics[DEPTH, 1, at, :] * east_rim[at, :],
            )
            for half in range(2):
                new = statics[SEA, half, at, :] * (
                    height[half, at, :] - (spread[half] + along(flux, half, b))
                )
                height[half, at, :] = new
                press[half, inner(b), :] = (0.5 * PRESS_RATE) * new + (
                    cosine * statics[COS, half, at, :] + sine * statics[SIN, half, at, :]
                )
        for b in range(blocks):
            at = span(b)
            slope = across(press[0, inner(b), :], press[1, inner(b), :])
            turn = rotation[at, :]
            for half in range(2):
                east_now = east[n, at, :] if half == 0 else east_rim[at, :]
                north_now = north[n, at, :] if half == 0 else north_rim[at, :]
                keep = statics[KEEP, half, at, :]
                east_new = keep * (east_now - slope[half] + turn * north_now)
                north_new = keep * (north_now - along(press, half, b) - turn * east_now)
                if half == 0:
                    east[n + 1, at, :] = east_new
                    north[n + 1, at, :] = north_new
                else:
                    east_rim[at, :] = east_new
                    north_rim[at, :] = north_new
                flux[half, inner(b), :] = statics[DEPTH, half, at, :] * north_new
        return carry

    lax.fori_loop(0, STEPS, forward, 0)

    start_copy.wait_recv()
    for b in range(blocks):
        at = span(b)
        sea = statics[SEA, 0, at, :]
        keep = statics[KEEP, 0, at, :]
        miss = sea * (height[0, at, :] - next_start[0, at, :])
        defect[0, at, :] = miss
        height[0, at, :] = miss
        end = east[STEPS, at, :]
        miss = sea * (end - next_start[1, at, :])
        defect[1, at, :] = miss
        east_part = keep * miss
        end_north = north[STEPS, at, :]
        miss = sea * (end_north - next_start[2, at, :])
        defect[2, at, :] = miss
        north_part = keep * miss
        total[at, :] = east_part * end + north_part * end_north
        grad[1, at, :] = east_part
        flux[0, inner(b), :] = north_part
    behind_copy = pltpu.make_async_remote_copy(
        src_ref=defect,
        dst_ref=behind,
        send_sem=behind_send,
        recv_sem=behind_recv,
        device_id=(ahead, cell),
        device_id_type=MESH,
    )
    behind_copy.start()
    defect_store = pltpu.make_async_copy(defect, defect_out.at[0], out_sem.at[0])
    defect_store.start()

    for relay in relays:
        relay.wait_recv()
    for b in range(blocks):
        at = span(b)
        sea = statics[SEA, 1, at, :]
        keep = statics[KEEP, 1, at, :]
        height[1, at, :] = sea * (height[1, at, :] - unpack_state(next_rim, 0, 0, b))
        east_rim[at, :] = keep * (east_rim[at, :] - unpack_state(next_rim, 0, 1, b))
        flux[1, inner(b), :] = keep * (north_rim[at, :] - unpack_state(next_rim, 0, 2, b))

    def adjoint_height(halves):
        for b in range(blocks):
            at = span(b)
            slope = across(grad[1, at, :], east_rim[at, :])
            for half in range(halves):
                new = statics[SEA, half, at, :] * (
                    height[half, at, :]
                    + (0.5 * PRESS_RATE) * (slope[half] + along(flux, half, b))
                )
                height[half, at, :] = new
                press[half, inner(b), :] = new

    def adjoint(i, carry):
        n = STEPS - 1 - i
        adjoint_height(2)
        for b in range(blocks):
            at = span(b)
            slope = across(press[0, inner(b), :], press[1, inner(b), :])
            turn = rotation[at, :]
            for half in range(2):
                east_part = grad[1, at, :] if half == 0 else east_rim[at, :]
                north_part = flux[half, inner(b), :]
                keep = statics[KEEP, half, at, :]
                depth = statics[DEPTH, half, at, :]
                east_new = keep * (east_part - turn * north_part + depth * slope[half])
                north_new = keep * (north_part + turn * east_part + depth * along(press, half, b))
                if half == 0:
                    grad[1, at, :] = east_new
                    total[at, :] = total[at, :] + (
                        east_new * east[n, at, :] + north_new * north[n, at, :]
                    )
                else:
                    east_rim[at, :] = east_new
                flux[half, inner(b), :] = north_new
        return carry

    lax.fori_loop(0, STEPS - 1, adjoint, 0)

    share = rows // slices
    for t in range(slices):
        shares[t] = total[t * share : (t + 1) * share, :]
    share_copies = []
    for step in range(1, slices):
        peer = lax.rem(me + step, slices)
        share_copies.append(
            pltpu.make_async_remote_copy(
                src_ref=shares.at[peer],
                dst_ref=share_in.at[step],
                send_sem=share_send.at[step],
                recv_sem=share_recv.at[step],
                device_id=(peer, cell),
                device_id_type=MESH,
            )
        )
    for copy in share_copies:
        copy.start()

    adjoint_height(2)
    behind_copy.wait_recv()
    for b in range(blocks):
        at = span(b)
        slope = across_body(press[0, inner(b), :], press[1, inner(b), :])
        turn = rotation[at, :]
        sea = statics[SEA, 0, at, :]
        depth = statics[DEPTH, 0, at, :]
        east_part = grad[1, at, :]
        north_part = flux[0, inner(b), :]
        grad[0, at, :] = height[0, at, :] - behind[0, at, :]
        grad[1, at, :] = (
            sea * (east_part - turn * north_part + depth * slope) - behind[1, at, :]
        )
        grad[2, at, :] = (
            sea * (north_part + turn * east_part + depth * along(press, 0, b))
            - behind[2, at, :]
        )
    grad_store = pltpu.make_async_copy(grad, grad_out.at[0], out_sem.at[1])
    grad_store.start()

    summed = shares[me]
    for step in range(1, slices):
        share_copies[step - 1].wait_recv()
        summed = summed + share_in[step]
    share_out[...] = summed * (-1.0 / slices)
    drag_store = pltpu.make_async_copy(share_out, drag_out, out_sem.at[2])
    drag_store.start()

    for copy in halos + [start_copy] + relays + [behind_copy] + share_copies:
        copy.wait_send()
    defect_store.wait()
    grad_store.wait()
    drag_store.wait()


def local(slices, cells, start_states, ocean_mask, depth_class, class_depth, drag_rate, tide_cos, tide_sin):
    rows, lanes = ocean_mask.shape
    assert lanes == LANES and rows == 4 * BLOCK and rows % slices == 0
    share = rows // slices

    def f32(*shape):
        return pltpu.VMEM(shape, jnp.float32)

    sems = pltpu.SemaphoreType.DMA
    hbm = pl.BlockSpec(memory_space=pl.ANY)
    wide = rows + 2 * PAD
    rim_rows = rows - BLOCK
    return pl.pallas_call(
        functools.partial(kernel, slices, cells),
        out_shape=(
            jax.ShapeDtypeStruct(start_states.shape, jnp.float32),
            jax.ShapeDtypeStruct(start_states.shape, jnp.float32),
            jax.ShapeDtypeStruct((share, lanes), jnp.float32),
        ),
        in_specs=[hbm, hbm, hbm, pl.BlockSpec(memory_space=pltpu.SMEM), hbm, hbm, hbm],
        out_specs=(hbm, hbm, hbm),
        scratch_shapes=[
            f32(3, rows, lanes),
            pltpu.VMEM((rows, lanes), jnp.int32),
            pltpu.VMEM((rows, lanes), jnp.int32),
            f32(rows, lanes),
            f32(2, rows, lanes),
            f32(5, 2, rows, lanes),
            f32(rows, lanes),
            f32(2 * STEPS, lanes),
            f32(2, rows, lanes),
            f32(STEPS + 1, rows, lanes),
            f32(STEPS + 1, rows, lanes),
            f32(rows, lanes),
            f32(rows, lanes),
            f32(2, wide, lanes),
            f32(2, wide, lanes),
            f32(2, rows + rim_rows, lanes),
            f32(2, rows + rim_rows, lanes),
            f32(2, rim_rows, lanes),
            f32(3, rows, lanes),
            f32(3, rows, lanes),
            f32(3, rows, lanes),
            f32(3, rows, lanes),
            f32(rows, lanes),
            f32(slices, share, lanes),
            f32(slices, share, lanes),
            f32(share, lanes),
            sems((6,)),
            sems((3,)),
            sems((2,)),
            sems((2,)),
            sems,
            sems,
            sems((2,)),
            sems((2,)),
            sems,
            sems,
            sems((slices,)),
            sems((slices,)),
        ],
        compiler_params=pltpu.CompilerParams(
            collective_id=0, has_side_effects=True, vmem_limit_bytes=32 * 1024 * 1024
        ),
    )(start_states, ocean_mask, depth_class, class_depth, drag_rate, tide_cos, tide_sin)


def solution(mesh):
    return jax.shard_map(
        functools.partial(local, mesh.shape["tm"], mesh.shape["cell"]),
        mesh=mesh,
        in_specs=(
            P("tm", None, None, "cell"),
            P(None, "cell"),
            P(None, "cell"),
            P(),
            P(None, "cell"),
            P(None, "cell"),
            P(None, "cell"),
        ),
        out_specs=(P("tm", None, None, "cell"), P("tm", None, None, "cell"), P("tm", "cell")),
        check_vma=False,
    )
```

time: 116 us -> 31.3 us (0.27)
  waiting for transfers between devices: 66.3 us -> 0 us
  Pallas kernels: 0 us -> 22.6 us
  other arithmetic: 16 us -> 0 us
  between operations: 15.9 us -> 0.66 us
  starting transfers between devices: 13.1 us -> 0 us
  local copies, waits for them, and re-layouts: 4.3 us -> 7.72 us
    ppermute x8 -> x0, waiting for transfers between devices: 35.3 us -> none  [the longest x3 20.3 us: with_halo(): lax.ppermute(lax.slice_in_dim(block, block.shape[dim] - width, None, axis...]
    reduce_scatter x1 -> x0, waiting for transfers between devices: 31 us -> none  [local(): lax.psum_scatter(drag_total, 'tm', scatter_dimension=0, tiled=True)]
    pallas_call x0 -> x1, Pallas kernels: none -> 22.6 us  [local(): pl.pallas_call(functools.partial(kernel, slices, cells), out_shape=(jax.S...]
    ppermute x8 -> x0, starting transfers between devices: 13 us -> none  [the longest x3 8.6 us: with_halo(): lax.ppermute(lax.slice_in_dim(block, 0, width, axis=dim), axis, backward)]
    mul x28 -> x0, other arithmetic: 7.13 us -> none  [the longest x8 2.11 us: adjoint_step(): east_part = mask_keep * adjoint[1]]
    unnamed x17, local copies, waits for them, and re-layouts: 3.18 us -> 7.72 us
    add x8 -> x0, other arithmetic: 2.18 us -> none  [advance_wide(): height_new + cropped(cosine * statics[3] + sine_now * statics[4], 1)]
    squeeze x8 -> x0, other arithmetic: 1.43 us -> none  [advance_wide(): sea_mask, depth_field, retain = (statics[0], statics[1], statics[2])]
  transfers between devices with their start and end apart: 9 -> 0, of which waited for: 7 -> 0; matrix products, arithmetic and copies ran while one was open for 1% -> 0% of each run, Pallas kernels for 0% -> 0%
where the time goes in v1:
time: 31.3 us; the launch traced here: 31 us
  Pallas kernels  22.6 us (72%)
  local copies, waits for them, and re-layouts  7.72 us (25%)
  between operations  0.66 us (2%)
    pallas_call x1, Pallas kernels, local(): pl.pallas_call(functools.partial(kernel, slices, cells), out_shape=(jax.S...  22.6 us
    unnamed x17, local copies, waits for them, and re-layouts  7.72 us

profile of v1, /device:TPU:0, one launch (start us, length us, event | category | flops | bytes accessed | tf_op | source)
XLA Modules:
  0.0 31.0 jit_solution(10985311324426897667)
XLA Ops:
  0.6 0.0 copy-start
  0.6 0.9 %copy-done = f32[1,3,128,128]{3,2,1,0:T(8,128)S(1)} copy-done((f32[1,3,128,128]{3,2,1,0:T(8,128)S(1)}, f32[1,3,128,128]{3,2,1,0:T(8,128)}, u32[]{:S(2)}) %copy-start) | copy-done | bytes 196632
  1.6 0.0 copy-start.1
  1.6 0.8 %copy-done.1 = s32[128,128]{1,0:T(8,128)S(1)} copy-done((s32[128,128]{1,0:T(8,128)S(1)}, s32[128,128]{1,0:T(8,128)}, u32[]{:S(2)}) %copy-start.1) | copy-done | bytes 65560
  2.4 0.0 copy-start.2
  2.4 0.8 %copy-done.2 = s32[128,128]{1,0:T(8,128)S(1)} copy-done((s32[128,128]{1,0:T(8,128)S(1)}, s32[128,128]{1,0:T(8,128)}, u32[]{:S(2)}) %copy-start.2) | copy-done | bytes 65560
  3.2 0.0 copy-start.3
  3.2 0.8 %copy-done.3 = f32[128,128]{1,0:T(8,128)S(1)} copy-done((f32[128,128]{1,0:T(8,128)S(1)}, f32[128,128]{1,0:T(8,128)}, u32[]{:S(2)}) %copy-start.3) | copy-done | bytes 65560
  4.1 0.0 copy-start.4
  4.1 0.8 %copy-done.4 = f32[128,128]{1,0:T(8,128)S(1)} copy-done((f32[128,128]{1,0:T(8,128)S(1)}, f32[128,128]{1,0:T(8,128)}, u32[]{:S(2)}) %copy-start.4) | copy-done | bytes 65560
  4.9 0.0 copy-start.5
  4.9 0.8 %copy-done.5 = f32[128,128]{1,0:T(8,128)S(1)} copy-done((f32[128,128]{1,0:T(8,128)S(1)}, f32[128,128]{1,0:T(8,128)}, u32[]{:S(2)}) %copy-start.5) | copy-done | bytes 65560
  5.8 0.0 copy-start.6
  5.8 0.7 %copy-done.6 = f32[8]{0:T(128)S(1)} copy-done((f32[8]{0:T(128)S(1)}, f32[8]{0:T(128)}, u32[]{:S(2)}) %copy-start.6) | copy-done | bytes 56
  6.4 22.6 %shard_map.94 = (f32[1,3,128,128]{3,2,1,0:T(8,128)S(1)}, f32[1,3,128,128]{3,2,1,0:T(8,128)S(1)}, f32[16,128]{1,0:T(8,128)S(1)}) custom-call(f32[1,3,128,128]{3,2,1,0:T(8,128)S(1)} %copy-done, s32[128,128]{1,0:T(8,128)S(1)} %copy-done.1, s32[128,128]{1,0:T(8,128)S(1)} %copy-done.2, f32[8]{0:T(128)S(1)} %copy-done.6, f32[128,128]{1,0:T(8,128)S(1)} %copy-done.3, ...), custom_call_target="tpu_custom_call" | custom-call | tf_op jit(solution)/shard_map/pallas_call | solution.py:445
  29.0 0.7 %copy.13 = f32[1,3,128,128]{3,2,1,0:T(8,128)} copy(f32[1,3,128,128]{3,2,1,0:T(8,128)S(1)} %get-tuple-element.6) | data formatting | bytes 393216
  29.7 0.7 %copy.14 = f32[1,3,128,128]{3,2,1,0:T(8,128)} copy(f32[1,3,128,128]{3,2,1,0:T(8,128)S(1)} %get-tuple-element.7) | data formatting | bytes 393216
  30.4 0.6 %copy.15 = f32[16,128]{1,0:T(8,128)} copy(f32[16,128]{1,0:T(8,128)S(1)} %get-tuple-element.8) | data formatting | bytes 16384
Async XLA Ops:
  0.6 0.9 %copy-start = (f32[1,3,128,128]{3,2,1,0:T(8,128)S(1)}, f32[1,3,128,128]{3,2,1,0:T(8,128)}, u32[]{:S(2)}) copy-start(f32[1,3,128,128]{3,2,1,0:T(8,128)} %start_ref.1) | copy-start | bytes 589828
  1.6 0.8 %copy-start.1 = (s32[128,128]{1,0:T(8,128)S(1)}, s32[128,128]{1,0:T(8,128)}, u32[]{:S(2)}) copy-start(s32[128,128]{1,0:T(8,128)} %mask_ref.1) | copy-start | bytes 196612
  2.4 0.8 %copy-start.2 = (s32[128,128]{1,0:T(8,128)S(1)}, s32[128,128]{1,0:T(8,128)}, u32[]{:S(2)}) copy-start(s32[128,128]{1,0:T(8,128)} %class_ref.1) | copy-start | bytes 196612
  3.2 0.8 %copy-start.3 = (f32[128,128]{1,0:T(8,128)S(1)}, f32[128,128]{1,0:T(8,128)}, u32[]{:S(2)}) copy-start(f32[128,128]{1,0:T(8,128)} %drag_ref.1) | copy-start | bytes 196612
  4.1 0.8 %copy-start.4 = (f32[128,128]{1,0:T(8,128)S(1)}, f32[128,128]{1,0:T(8,128)}, u32[]{:S(2)}) copy-start(f32[128,128]{1,0:T(8,128)} %cos_ref.1) | copy-start | bytes 196612
  4.9 0.8 %copy-start.5 = (f32[128,128]{1,0:T(8,128)S(1)}, f32[128,128]{1,0:T(8,128)}, u32[]{:S(2)}) copy-start(f32[128,128]{1,0:T(8,128)} %sin_ref.1) | copy-start | bytes 196612
  5.8 0.7 %copy-start.6 = (f32[8]{0:T(128)S(1)}, f32[8]{0:T(128)}, u32[]{:S(2)}) copy-start(f32[8]{0:T(128)} %table_ref.1) | copy-start | bytes 100

commit v2 on v1

v2 whole, which is shorter than its diff:
```python
import functools
import math

import jax
import jax.numpy as jnp
from jax import lax
from jax.experimental import pallas as pl
from jax.experimental.pallas import tpu as pltpu
from jax.sharding import PartitionSpec as P

STEPS = 8
FLUX_RATE = 0.7
PRESS_RATE = 0.7
ROTATION_RATE = 0.15

LANES = 128
RIM = 4 * STEPS
PAD = 8
BLOCK = 32
MESH = pl.DeviceIdType.MESH

SEA, KEEP, DEPTH, COS, SIN = range(5)


def kernel(
    slices,
    cells,
    start_ref,
    mask_ref,
    class_ref,
    table_ref,
    drag_ref,
    cos_ref,
    sin_ref,
    defect_out,
    grad_out,
    drag_out,
    start,
    mask,
    classes,
    drag,
    tides,
    statics,
    rotation,
    trig,
    height,
    east,
    north,
    adjoint_east,
    flux,
    press,
    packed,
    arrived,
    next_rim,
    next_start,
    defect,
    behind,
    grad,
    total,
    shares,
    share_in,
    share_out,
    in_sem,
    out_sem,
    halo_send,
    halo_recv,
    next_send,
    next_recv,
    rim_send,
    rim_recv,
    behind_send,
    behind_recv,
    share_send,
    share_recv,
):
    rows = mask.shape[0]
    blocks = rows // BLOCK
    me = lax.axis_index("tm")
    cell = lax.axis_index("cell")
    ahead = lax.rem(me + 1, slices)
    back = lax.rem(me + slices - 1, slices)
    east_cell = lax.rem(cell + 1, cells)
    west_cell = lax.rem(cell + cells - 1, cells)

    barrier = pltpu.get_barrier_semaphore()
    for other in (west_cell, east_cell):
        pl.semaphore_signal(barrier, inc=1, device_id=(me, other), device_id_type=MESH)
    for step in range(1, slices):
        peer = lax.rem(me + step, slices)
        pl.semaphore_signal(barrier, inc=1, device_id=(peer, cell), device_id_type=MESH)

    loads = [
        pltpu.make_async_copy(source, target, in_sem.at[i])
        for i, (source, target) in enumerate(
            (
                (mask_ref, mask),
                (class_ref, classes),
                (drag_ref, drag),
                (cos_ref, tides.at[0]),
                (sin_ref, tides.at[1]),
                (start_ref.at[0], start),
            )
        )
    ]
    for load in loads:
        load.start()
    for load in loads:
        load.wait()

    lane = lax.broadcasted_iota(jnp.int32, (BLOCK, LANES), 1)
    slot = lane // RIM

    def span(b):
        return pl.ds(b * BLOCK, BLOCK)

    def across(value):
        return pltpu.roll(value, LANES - 1, 1) - pltpu.roll(value, 1, 1)

    def along(ref, half, b):
        upper = ref[half, pl.ds(PAD + b * BLOCK + 1, BLOCK), :]
        lower = ref[half, pl.ds(PAD + b * BLOCK - 1, BLOCK), :]
        return upper - lower

    def inner(b):
        return pl.ds(PAD + b * BLOCK, BLOCK)

    def turned(value, by):
        return value if by % 4 == 0 else pltpu.roll(value, by % 4 * RIM, 1)

    def pack(parts):
        west = parts[0]
        east_side = turned(parts[0], 2)
        for f in range(1, 4):
            west = jnp.where(slot == f, turned(parts[f], f), west)
            east_side = jnp.where(slot == (f + 1) % 4, turned(parts[f], f - 2), east_side)
        return west, east_side

    def own_edges(value):
        return jnp.where(slot == 3, value, turned(value, 2))

    for b in range(blocks):
        at = span(b)
        sea = mask[at, :].astype(jnp.float32)
        depth = jnp.zeros((BLOCK, LANES), jnp.float32)
        kind = classes[at, :]
        for c in range(table_ref.shape[0]):
            depth = jnp.where(kind == c, table_ref[c], depth)
        depth = (0.5 * FLUX_RATE) * depth
        keep = sea / (1.0 + drag[at, :])
        cosine = (0.5 * PRESS_RATE) * tides[0, at, :]
        sine = (0.5 * PRESS_RATE) * tides[1, at, :]
        fields = (sea, keep, depth, cosine, sine)
        for f in range(5):
            statics[f, 0, at, :] = fields[f]
        west, east_side = pack(fields[1:])
        packed[0, at, :] = west
        packed[1, at, :] = east_side
    for b in range(blocks - 1):
        parts = [start[f, span(b), :] for f in range(3)]
        parts.append(start[b, span(blocks - 1), :])
        west, east_side = pack(parts)
        packed[0, pl.ds(rows + b * BLOCK, BLOCK), :] = west
        packed[1, pl.ds(rows + b * BLOCK, BLOCK), :] = east_side

    pl.semaphore_wait(barrier, slices + 1)

    halos = [
        pltpu.make_async_remote_copy(
            src_ref=packed.at[side],
            dst_ref=arrived.at[side],
            send_sem=halo_send.at[side],
            recv_sem=halo_recv.at[side],
            device_id=(me, other),
            device_id_type=MESH,
        )
        for side, other in ((0, west_cell), (1, east_cell))
    ]
    for halo in halos:
        halo.start()
    start_copy = pltpu.make_async_remote_copy(
        src_ref=start,
        dst_ref=next_start,
        send_sem=next_send,
        recv_sem=next_recv,
        device_id=(back, cell),
        device_id_type=MESH,
    )
    start_copy.start()

    latitude = lax.broadcasted_iota(jnp.int32, (rows, LANES), 0).astype(jnp.float32)
    latitude = math.pi * ((latitude + 0.5) / rows - 0.5)
    rotation[...] = ROTATION_RATE * jnp.sin(latitude)
    unit = 2.0 * math.pi / (slices * STEPS)
    number = lax.broadcasted_iota(jnp.int32, (STEPS, LANES), 0) + me * STEPS
    phase = number.astype(jnp.float32) * unit
    trig[0:STEPS, :] = jnp.cos(phase)
    trig[STEPS : 2 * STEPS, :] = jnp.sin(phase)
    blank = jnp.zeros((PAD, LANES), jnp.float32)
    for ref in (flux, press):
        for half in range(2):
            ref[half, 0:PAD, :] = blank
            ref[half, PAD + rows : 2 * PAD + rows, :] = blank
    for b in range(blocks):
        at = span(b)
        sea = statics[SEA, 0, at, :]
        height[0, at, :] = sea * start[0, at, :]
        east[0, 0, at, :] = sea * start[1, at, :]
        north_now = sea * start[2, at, :]
        north[0, 0, at, :] = north_now
        flux[0, inner(b), :] = statics[DEPTH, 0, at, :] * north_now

    def forward(half, n, carry):
        cosine = trig[pl.ds(n, 1), :]
        sine = trig[pl.ds(STEPS + n, 1), :]
        for b in range(blocks):
            at = span(b)
            spread = across(statics[DEPTH, half, at, :] * east[n, half, at, :])
            new = statics[SEA, half, at, :] * (
                height[half, at, :] - (spread + along(flux, half, b))
            )
            height[half, at, :] = new
            press[half, inner(b), :] = (0.5 * PRESS_RATE) * new + (
                cosine * statics[COS, half, at, :] + sine * statics[SIN, half, at, :]
            )
        for b in range(blocks):
            at = span(b)
            turn = rotation[at, :]
            east_now = east[n, half, at, :]
            north_now = north[n, half, at, :]
            keep = statics[KEEP, half, at, :]
            north_new = keep * (north_now - along(press, half, b) - turn * east_now)
            east[n + 1, half, at, :] = keep * (
                east_now - across(press[half, inner(b), :]) + turn * north_now
            )
            north[n + 1, half, at, :] = north_new
            flux[half, inner(b), :] = statics[DEPTH, half, at, :] * north_new
        return carry

    lax.fori_loop(0, STEPS, functools.partial(forward, 0), 0)

    for halo in halos:
        halo.wait_recv()
    relays = [
        pltpu.make_async_remote_copy(
            src_ref=arrived.at[side, pl.ds(rows, rows - BLOCK)],
            dst_ref=next_rim.at[side],
            send_sem=rim_send.at[side],
            recv_sem=rim_recv.at[side],
            device_id=(back, cell),
            device_id_type=MESH,
        )
        for side in range(2)
    ]
    for relay in relays:
        relay.start()

    def unpack(ref, at, f, own):
        rims = turned(
            jnp.where(slot == f, ref[0, at, :], ref[1, at, :]),
            -f,
        )
        return jnp.where(slot < 2, rims, own_edges(own))

    def unpack_state(ref, offset, f, b, own):
        if b < blocks - 1:
            return unpack(ref, pl.ds(offset + b * BLOCK, BLOCK), f, own)
        return unpack(ref, pl.ds(offset + f * BLOCK, BLOCK), 3, own)

    for b in range(blocks):
        at = span(b)
        fields = [unpack(arrived, at, f, statics[f + 1, 0, at, :]) for f in range(4)]
        sea = jnp.where(fields[0] > 0.0, 1.0, 0.0)
        statics[SEA, 1, at, :] = sea
        for f in range(4):
            statics[f + 1, 1, at, :] = fields[f]
        state = [sea * unpack_state(arrived, rows, f, b, start[f, at, :]) for f in range(3)]
        height[1, at, :] = state[0]
        east[0, 1, at, :] = state[1]
        north[0, 1, at, :] = state[2]
        flux[1, inner(b), :] = fields[1] * state[2]

    lax.fori_loop(0, STEPS, functools.partial(forward, 1), 0)

    lost = 2 * STEPS
    outer = (lane < lost) | (lane >= LANES - lost)

    def whole(body, edges):
        return jnp.where(outer, jnp.where(slot == 0, turned(edges, 2), edges), body)

    def edges_from(body, edges):
        inward = (lane >= 2 * RIM + lost) & (lane < LANES - lost)
        return jnp.where(inward, own_edges(body), edges)

    start_copy.wait_recv()
    for b in range(blocks):
        at = span(b)
        sea = statics[SEA, 0, at, :]
        for f in range(3):
            ends = [
                height[half, at, :] if f == 0 else (east, north)[f - 1][STEPS, half, at, :]
                for half in range(2)
            ]
            defect[f, at, :] = sea * (whole(*ends) - next_start[f, at, :])
    behind_copy = pltpu.make_async_remote_copy(
        src_ref=defect,
        dst_ref=behind,
        send_sem=behind_send,
        recv_sem=behind_recv,
        device_id=(ahead, cell),
        device_id_type=MESH,
    )
    behind_copy.start()
    defect_store = pltpu.make_async_copy(defect, defect_out.at[0], out_sem.at[0])
    defect_store.start()

    for relay in relays:
        relay.wait_recv()
    for b in range(blocks):
        at = span(b)
        for half in range(2):
            keep = statics[KEEP, half, at, :]
            misses = []
            for f in range(3):
                miss = defect[f, at, :]
                if half == 1:
                    end = height[1, at, :] if f == 0 else (east, north)[f - 1][STEPS, 1, at, :]
                    target = unpack_state(next_rim, 0, f, b, next_start[f, at, :])
                    miss = edges_from(miss, statics[SEA, 1, at, :] * (end - target))
                misses.append(miss)
            east_part = keep * misses[1]
            north_part = keep * misses[2]
            height[half, at, :] = misses[0]
            adjoint_east[half, at, :] = east_part
            flux[half, inner(b), :] = north_part
            total[half, at, :] = (
                east_part * east[STEPS, half, at, :] + north_part * north[STEPS, half, at, :]
            )

    def adjoint_height(half):
        for b in range(blocks):
            at = span(b)
            slope = across(adjoint_east[half, at, :]) + along(flux, half, b)
            new = statics[SEA, half, at, :] * (height[half, at, :] + (0.5 * PRESS_RATE) * slope)
            height[half, at, :] = new
            press[half, inner(b), :] = new

    def adjoint_flow(half, b):
        at = span(b)
        turn = rotation[at, :]
        depth = statics[DEPTH, half, at, :]
        east_part = adjoint_east[half, at, :]
        north_part = flux[half, inner(b), :]
        slope = across(press[half, inner(b), :])
        return (
            east_part - turn * north_part + depth * slope,
            north_part + turn * east_part + depth * along(press, half, b),
        )

    def adjoint(i, carry):
        n = STEPS - 1 - i
        for half in range(2):
            adjoint_height(half)
        for half in range(2):
            for b in range(blocks):
                at = span(b)
                east_new, north_new = adjoint_flow(half, b)
                keep = statics[KEEP, half, at, :]
                east_new = keep * east_new
                north_new = keep * north_new
                adjoint_east[half, at, :] = east_new
                flux[half, inner(b), :] = north_new
                total[half, at, :] = total[half, at, :] + (
                    east_new * east[n, half, at, :] + north_new * north[n, half, at, :]
                )
        return carry

    lax.fori_loop(0, STEPS - 1, adjoint, 0)

    for b in range(blocks):
        at = span(b)
        total[0, at, :] = whole(total[0, at, :], total[1, at, :])
    share = rows // slices
    for t in range(slices):
        shares[t] = total[0, t * share : (t + 1) * share, :]
    share_copies = []
    for step in range(1, slices):
        peer = lax.rem(me + step, slices)
        share_copies.append(
            pltpu.make_async_remote_copy(
                src_ref=shares.at[peer],
                dst_ref=share_in.at[step],
                send_sem=share_send.at[step],
                recv_sem=share_recv.at[step],
                device_id=(peer, cell),
                device_id_type=MESH,
            )
        )
    for copy in share_copies:
        copy.start()

    for half in range(2):
        adjoint_height(half)
    behind_copy.wait_recv()
    for b in range(blocks):
        at = span(b)
        sea = statics[SEA, 0, at, :]
        body = adjoint_flow(0, b)
        edges = adjoint_flow(1, b)
        grad[0, at, :] = whole(height[0, at, :], height[1, at, :]) - behind[0, at, :]
        for f in range(2):
            grad[f + 1, at, :] = sea * whole(body[f], edges[f]) - behind[f + 1, at, :]
    grad_store = pltpu.make_async_copy(grad, grad_out.at[0], out_sem.at[1])
    grad_store.start()

    summed = shares[me]
    for step in range(1, slices):
        share_copies[step - 1].wait_recv()
        summed = summed + share_in[step]
    share_out[...] = summed * (-1.0 / slices)
    drag_store = pltpu.make_async_copy(share_out, drag_out, out_sem.at[2])
    drag_store.start()

    for copy in halos + [start_copy] + relays + [behind_copy] + share_copies:
        copy.wait_send()
    defect_store.wait()
    grad_store.wait()
    drag_store.wait()


def handed_over(*refs):
    sems = refs[6]
    copies = [pltpu.make_async_copy(refs[i], refs[3 + i], sems.at[i]) for i in range(3)]
    for copy in copies:
        copy.start()
    for copy in copies:
        copy.wait()


def local(slices, cells, start_states, ocean_mask, depth_class, class_depth, drag_rate, tide_cos, tide_sin):
    rows, lanes = ocean_mask.shape
    assert lanes == LANES and rows == 4 * BLOCK and rows % slices == 0
    share = rows // slices

    def f32(*shape):
        return pltpu.VMEM(shape, jnp.float32)

    sems = pltpu.SemaphoreType.DMA
    hbm = pl.BlockSpec(memory_space=pl.ANY)
    wide = rows + 2 * PAD
    rim_rows = rows - BLOCK
    results = pl.pallas_call(
        functools.partial(kernel, slices, cells),
        out_shape=(
            jax.ShapeDtypeStruct(start_states.shape, jnp.float32),
            jax.ShapeDtypeStruct(start_states.shape, jnp.float32),
            jax.ShapeDtypeStruct((share, lanes), jnp.float32),
        ),
        in_specs=[hbm, hbm, hbm, pl.BlockSpec(memory_space=pltpu.SMEM), hbm, hbm, hbm],
        out_specs=(hbm, hbm, hbm),
        scratch_shapes=[
            f32(3, rows, lanes),
            pltpu.VMEM((rows, lanes), jnp.int32),
            pltpu.VMEM((rows, lanes), jnp.int32),
            f32(rows, lanes),
            f32(2, rows, lanes),
            f32(5, 2, rows, lanes),
            f32(rows, lanes),
            f32(2 * STEPS, lanes),
            f32(2, rows, lanes),
            f32(STEPS + 1, 2, rows, lanes),
            f32(STEPS + 1, 2, rows, lanes),
            f32(2, rows, lanes),
            f32(2, wide, lanes),
            f32(2, wide, lanes),
            f32(2, rows + rim_rows, lanes),
            f32(2, rows + rim_rows, lanes),
            f32(2, rim_rows, lanes),
            f32(3, rows, lanes),
            f32(3, rows, lanes),
            f32(3, rows, lanes),
            f32(3, rows, lanes),
            f32(2, rows, lanes),
            f32(slices, share, lanes),
            f32(slices, share, lanes),
            f32(share, lanes),
            sems((6,)),
            sems((3,)),
            sems((2,)),
            sems((2,)),
            sems,
            sems,
            sems((2,)),
            sems((2,)),
            sems,
            sems,
            sems((slices,)),
            sems((slices,)),
        ],
        compiler_params=pltpu.CompilerParams(
            collective_id=0, has_side_effects=True, vmem_limit_bytes=60 * 1024 * 1024
        ),
    )(start_states, ocean_mask, depth_class, class_depth, drag_rate, tide_cos, tide_sin)
    return pl.pallas_call(
        handed_over,
        out_shape=tuple(jax.ShapeDtypeStruct(r.shape, r.dtype) for r in results),
        in_specs=[hbm] * 3,
        out_specs=(hbm,) * 3,
        scratch_shapes=[sems((3,))],
        compiler_params=pltpu.CompilerParams(vmem_limit_bytes=60 * 1024 * 1024),
    )(*results)


def solution(mesh):
    return jax.shard_map(
        functools.partial(local, mesh.shape["tm"], mesh.shape["cell"]),
        mesh=mesh,
        in_specs=(
            P("tm", None, None, "cell"),
            P(None, "cell"),
            P(None, "cell"),
            P(),
            P(None, "cell"),
            P(None, "cell"),
            P(None, "cell"),
        ),
        out_specs=(P("tm", None, None, "cell"), P("tm", None, None, "cell"), P("tm", "cell")),
        check_vma=False,
    )
```

time: 31.3 us -> 37.6 us (1.20)
  Pallas kernels: 22.6 us -> 36.8 us
  local copies, waits for them, and re-layouts: 7.72 us -> 0 us
    pallas_call x0 -> x1, Pallas kernels: none -> 13.3 us  [local(): pl.pallas_call(handed_over, out_shape=tuple((jax.ShapeDtypeStruct(r.shape...]
    unnamed x17 -> x0, local copies, waits for them, and re-layouts: 7.72 us -> none
    pallas_call x1, Pallas kernels: 22.6 us -> 23.5 us  [local(): pl.pallas_call(functools.partial(kernel, slices, cells), out_shape=(jax.S...]
where the time goes in v2:
time: 37.6 us; the launch traced here: 37.4 us
  Pallas kernels  36.8 us (98%)
  between operations  0.64 us (2%)
    pallas_call x1, Pallas kernels, local(): pl.pallas_call(functools.partial(kernel, slices, cells), out_shape=(jax.S...  23.5 us
    pallas_call x1, Pallas kernels, local(): pl.pallas_call(handed_over, out_shape=tuple((jax.ShapeDtypeStruct(r.shape...  13.3 us

profile of v2, /device:TPU:0, one launch (start us, length us, event | category | flops | bytes accessed | tf_op | source)
XLA Modules:
  0.0 37.4 jit_solution(1572146557904300396)
XLA Ops:
  0.6 23.5 %shard_map.94 = (f32[1,3,128,128]{3,2,1,0:T(8,128)}, f32[1,3,128,128]{3,2,1,0:T(8,128)}, f32[16,128]{1,0:T(8,128)}) custom-call(f32[1,3,128,128]{3,2,1,0:T(8,128)} %start_ref.1, s32[128,128]{1,0:T(8,128)} %mask_ref.1, s32[128,128]{1,0:T(8,128)} %class_ref.1, f32[8]{0:T(128)} %table_ref.1, f32[128,128]{1,0:T(8,128)} %drag_ref.1, f32[128,128]{1,0:T(8,128)} %cos_ref.1, ...), custom_call_target="tpu_custom_call" | custom-call | tf_op jit(solution)/shard_map/pallas_call | solution.py:451
  24.1 13.3 %shard_map.95 = (f32[1,3,128,128]{3,2,1,0:T(8,128)}, f32[1,3,128,128]{3,2,1,0:T(8,128)}, f32[16,128]{1,0:T(8,128)}) custom-call(f32[1,3,128,128]{3,2,1,0:T(8,128)} %get-tuple-element.6.refs_0_, f32[1,3,128,128]{3,2,1,0:T(8,128)} %get-tuple-element.7.refs_1_, f32[16,128]{1,0:T(8,128)} %get-tuple-element.8.refs_2_), custom_call_target="tpu_custom_call" | custom-call | tf_op jit(solution)/shard_map/pallas_call | solution.py:503

commit v3 on v2

--- a/solution.py
+++ b/solution.py
@@ -28,7 +28,7 @@
     start_ref,
     mask_ref,
     class_ref,
-    table_ref,
+    depths_ref,
     drag_ref,
     cos_ref,
     sin_ref,
@@ -38,6 +38,7 @@
     start,
     mask,
     classes,
+    table,
     drag,
     tides,
     statics,
@@ -62,6 +63,8 @@
     share_out,
     in_sem,
     out_sem,
+    piece_send,
+    piece_recv,
     halo_send,
     halo_recv,
     next_send,
@@ -95,6 +98,7 @@
             (
                 (mask_ref, mask),
                 (class_ref, classes),
+                (depths_ref, table),
                 (drag_ref, drag),
                 (cos_ref, tides.at[0]),
                 (sin_ref, tides.at[1]),
@@ -143,8 +147,8 @@
         sea = mask[at, :].astype(jnp.float32)
         depth = jnp.zeros((BLOCK, LANES), jnp.float32)
         kind = classes[at, :]
-        for c in range(table_ref.shape[0]):
-            depth = jnp.where(kind == c, table_ref[c], depth)
+        for c in range(table.shape[0]):
+            depth = jnp.where(kind == c, table[c], depth)
         depth = (0.5 * FLUX_RATE) * depth
         keep = sea / (1.0 + drag[at, :])
         cosine = (0.5 * PRESS_RATE) * tides[0, at, :]
@@ -164,19 +168,36 @@
 
     pl.semaphore_wait(barrier, slices + 1)
 
+    group = math.gcd(slices, 8)
+    piece = rows // group
+    rank = lax.rem(me, group)
+    piece_rows = pl.ds(pl.multiple_of(rank * piece, piece), piece)
+    sides = ((0, west_cell), (1, east_cell))
+    pieces = [
+        pltpu.make_async_remote_copy(
+            src_ref=packed.at[side, piece_rows],
+            dst_ref=arrived.at[side, piece_rows],
+            send_sem=piece_send.at[side, 0],
+            recv_sem=piece_recv.at[side, 0],
+            device_id=(me, other),
+            device_id_type=MESH,
+        )
+        for side, other in sides
+    ]
+    state_rows = pl.ds(rows, rows - BLOCK)
     halos = [
         pltpu.make_async_remote_copy(
-            src_ref=packed.at[side],
-            dst_ref=arrived.at[side],
+            src_ref=packed.at[side, state_rows],
+            dst_ref=arrived.at[side, state_rows],
             send_sem=halo_send.at[side],
             recv_sem=halo_recv.at[side],
             device_id=(me, other),
             device_id_type=MESH,
         )
-        for side, other in ((0, west_cell), (1, east_cell))
+        for side, other in sides
     ]
-    for halo in halos:
-        halo.start()
+    for copy in pieces + halos:
+        copy.start()
     start_copy = pltpu.make_async_remote_copy(
         src_ref=start,
         dst_ref=next_start,
@@ -236,6 +257,22 @@
             flux[half, inner(b), :] = statics[DEPTH, half, at, :] * north_new
         return carry
 
+    shared = []
+    for side in range(2):
+        pieces[side].wait_recv()
+        for step in range(1, group):
+            shared.append(
+                pltpu.make_async_remote_copy(
+                    src_ref=arrived.at[side, piece_rows],
+                    dst_ref=arrived.at[side, piece_rows],
+                    send_sem=piece_send.at[side, step],
+                    recv_sem=piece_recv.at[side, step],
+                    device_id=(me - rank + lax.rem(rank + step, group), cell),
+                    device_id_type=MESH,
+                )
+            )
+            shared[-1].start()
+
     lax.fori_loop(0, STEPS, functools.partial(forward, 0), 0)
 
     for halo in halos:
@@ -253,6 +290,9 @@
     ]
     for relay in relays:
         relay.start()
+
+    for copy in shared:
+        copy.wait_recv()
 
     def unpack(ref, at, f, own):
         rims = turned(
@@ -420,7 +460,7 @@
     drag_store = pltpu.make_async_copy(share_out, drag_out, out_sem.at[2])
     drag_store.start()
 
-    for copy in halos + [start_copy] + relays + [behind_copy] + share_copies:
+    for copy in pieces + shared + halos + [start_copy] + relays + [behind_copy] + share_copies:
         copy.wait_send()
     defect_store.wait()
     grad_store.wait()
@@ -436,7 +476,8 @@
         copy.wait()
 
 
-def local(slices, cells, start_states, ocean_mask, depth_class, class_depth, drag_rate, tide_cos, tide_sin):
+def local(slices, cells, *operands):
+    start_states, ocean_mask, _, class_depth = operands[:4]
     rows, lanes = ocean_mask.shape
     assert lanes == LANES and rows == 4 * BLOCK and rows % slices == 0
     share = rows // slices
@@ -445,22 +486,20 @@
         return pltpu.VMEM(shape, jnp.float32)
 
     sems = pltpu.SemaphoreType.DMA
-    hbm = pl.BlockSpec(memory_space=pl.ANY)
+    hbm = pl.BlockSpec(memory_space=pltpu.HBM)
+    left = pl.BlockSpec(memory_space=pl.ANY)
     wide = rows + 2 * PAD
     rim_rows = rows - BLOCK
     results = pl.pallas_call(
         functools.partial(kernel, slices, cells),
-        out_shape=(
-            jax.ShapeDtypeStruct(start_states.shape, jnp.float32),
-            jax.ShapeDtypeStruct(start_states.shape, jnp.float32),
-            jax.ShapeDtypeStruct((share, lanes), jnp.float32),
-        ),
-        in_specs=[hbm, hbm, hbm, pl.BlockSpec(memory_space=pltpu.SMEM), hbm, hbm, hbm],
-        out_specs=(hbm, hbm, hbm),
+        out_shape=(f32(*start_states.shape), f32(*start_states.shape), f32(share, lanes)),
+        in_specs=[hbm] * 7,
+        out_specs=(left,) * 3,
         scratch_shapes=[
             f32(3, rows, lanes),
             pltpu.VMEM((rows, lanes), jnp.int32),
             pltpu.VMEM((rows, lanes), jnp.int32),
+            pltpu.SMEM(class_depth.shape, jnp.float32),
             f32(rows, lanes),
             f32(2, rows, lanes),
             f32(5, 2, rows, lanes),
@@ -483,8 +522,10 @@
             f32(slices, share, lanes),
             f32(slices, share, lanes),
             f32(share, lanes),
-            sems((6,)),
+            sems((7,)),
             sems((3,)),
+            sems((2, math.gcd(slices, 8))),
+            sems((2, math.gcd(slices, 8))),
             sems((2,)),
             sems((2,)),
             sems,
@@ -497,16 +538,18 @@
             sems((slices,)),
         ],
         compiler_params=pltpu.CompilerParams(
-            collective_id=0, has_side_effects=True, vmem_limit_bytes=60 * 1024 * 1024
+            collective_id=0, has_side_effects=True, vmem_limit_bytes=32 * 1024 * 1024
         ),
-    )(start_states, ocean_mask, depth_class, class_depth, drag_rate, tide_cos, tide_sin)
+    )(
+        *(pltpu.with_memory_space_constraint(x, pltpu.HBM) for x in operands),
+    )
     return pl.pallas_call(
         handed_over,
         out_shape=tuple(jax.ShapeDtypeStruct(r.shape, r.dtype) for r in results),
-        in_specs=[hbm] * 3,
+        in_specs=[left] * 3,
         out_specs=(hbm,) * 3,
         scratch_shapes=[sems((3,))],
-        compiler_params=pltpu.CompilerParams(vmem_limit_bytes=60 * 1024 * 1024),
+        compiler_params=pltpu.CompilerParams(vmem_limit_bytes=16 * 1024 * 1024),
     )(*results)
 
 

time: 37.6 us -> 22.3 us (0.59)
  Pallas kernels: 36.8 us -> 21.5 us
    pallas_call x1, Pallas kernels: 13.3 us -> 0.77 us  [local(): pl.pallas_call(handed_over, out_shape=tuple((jax.ShapeDtypeStruct(r.shape...]
    pallas_call x1, Pallas kernels: 23.5 us -> 20.8 us  [local(): pl.pallas_call(functools.partial(kernel, slices, cells), out_shape=(f32(*...]
where the time goes in v3:
time: 22.3 us; the launch traced here: 22.2 us
  Pallas kernels  21.5 us (96%)
  between operations  0.64 us (3%)
    pallas_call x1, Pallas kernels, local(): pl.pallas_call(functools.partial(kernel, slices, cells), out_shape=(f32(*...  20.8 us
    pallas_call x1, Pallas kernels, local(): pl.pallas_call(handed_over, out_shape=tuple((jax.ShapeDtypeStruct(r.shape...  0.77 us

profile of v3, /device:TPU:0, one launch (start us, length us, event | category | flops | bytes accessed | tf_op | source)
XLA Modules:
  0.0 22.2 jit_solution(9037511133944002916)
XLA Ops:
  0.6 20.8 %shard_map.94 = (f32[1,3,128,128]{3,2,1,0:T(8,128)S(1)}, f32[1,3,128,128]{3,2,1,0:T(8,128)S(1)}, f32[16,128]{1,0:T(8,128)S(1)}) custom-call(f32[1,3,128,128]{3,2,1,0:T(8,128)} %start_ref.1, s32[128,128]{1,0:T(8,128)} %mask_ref.1, s32[128,128]{1,0:T(8,128)} %class_ref.1, f32[8]{0:T(128)} %depths_ref.1, f32[128,128]{1,0:T(8,128)} %drag_ref.1, ...), custom_call_target="tpu_custom_call" | custom-call | tf_op jit(solution)/shard_map/pallas_call | solution.py:493
  21.4 0.8 %shard_map.95 = (f32[1,3,128,128]{3,2,1,0:T(8,128)}, f32[1,3,128,128]{3,2,1,0:T(8,128)}, f32[16,128]{1,0:T(8,128)}) custom-call(f32[1,3,128,128]{3,2,1,0:T(8,128)S(1)} %get-tuple-element.6.refs_0_, f32[1,3,128,128]{3,2,1,0:T(8,128)S(1)} %get-tuple-element.7.refs_1_, f32[16,128]{1,0:T(8,128)S(1)} %get-tuple-element.8.refs_2_), custom_call_target="tpu_custom_call" | custom-call | tf_op jit(solution)/shard_map/pallas_call | solution.py:546

commit v4 on v3

--- a/solution.py
+++ b/solution.py
@@ -12,6 +12,8 @@
 FLUX_RATE = 0.7
 PRESS_RATE = 0.7
 ROTATION_RATE = 0.15
+
+SCALE = 0.5 * PRESS_RATE
 
 LANES = 128
 RIM = 4 * STEPS
@@ -52,6 +54,7 @@
     press,
     packed,
     arrived,
+    own_rim,
     next_rim,
     next_start,
     defect,
@@ -60,7 +63,6 @@
     total,
     shares,
     share_in,
-    share_out,
     in_sem,
     out_sem,
     piece_send,
@@ -108,8 +110,6 @@
     ]
     for load in loads:
         load.start()
-    for load in loads:
-        load.wait()
 
     lane = lax.broadcasted_iota(jnp.int32, (BLOCK, LANES), 1)
     slot = lane // RIM
@@ -142,6 +142,16 @@
     def own_edges(value):
         return jnp.where(slot == 3, value, turned(value, 2))
 
+    loads[-1].wait()
+    for b in range(blocks - 1):
+        parts = [start[f, span(b), :] for f in range(3)]
+        parts.append(start[b, span(blocks - 1), :])
+        west, east_side = pack(parts)
+        packed[0, pl.ds(rows + b * BLOCK, BLOCK), :] = west
+        packed[1, pl.ds(rows + b * BLOCK, BLOCK), :] = east_side
+
+    for load in loads[:-1]:
+        load.wait()
     for b in range(blocks):
         at = span(b)
         sea = mask[at, :].astype(jnp.float32)
@@ -149,23 +159,16 @@
         kind = classes[at, :]
         for c in range(table.shape[0]):
             depth = jnp.where(kind == c, table[c], depth)
-        depth = (0.5 * FLUX_RATE) * depth
+        depth = (0.5 * FLUX_RATE * SCALE) * depth
         keep = sea / (1.0 + drag[at, :])
-        cosine = (0.5 * PRESS_RATE) * tides[0, at, :]
-        sine = (0.5 * PRESS_RATE) * tides[1, at, :]
+        cosine = tides[0, at, :]
+        sine = tides[1, at, :]
         fields = (sea, keep, depth, cosine, sine)
         for f in range(5):
             statics[f, 0, at, :] = fields[f]
         west, east_side = pack(fields[1:])
         packed[0, at, :] = west
         packed[1, at, :] = east_side
-    for b in range(blocks - 1):
-        parts = [start[f, span(b), :] for f in range(3)]
-        parts.append(start[b, span(blocks - 1), :])
-        west, east_side = pack(parts)
-        packed[0, pl.ds(rows + b * BLOCK, BLOCK), :] = west
-        packed[1, pl.ds(rows + b * BLOCK, BLOCK), :] = east_side
-
     pl.semaphore_wait(barrier, slices + 1)
 
     group = math.gcd(slices, 8)
@@ -225,14 +228,15 @@
         at = span(b)
         sea = statics[SEA, 0, at, :]
         height[0, at, :] = sea * start[0, at, :]
-        east[0, 0, at, :] = sea * start[1, at, :]
-        north_now = sea * start[2, at, :]
+        speed = (1.0 / SCALE) * sea
+        east[0, 0, at, :] = speed * start[1, at, :]
+        north_now = speed * start[2, at, :]
         north[0, 0, at, :] = north_now
         flux[0, inner(b), :] = statics[DEPTH, 0, at, :] * north_now
 
-    def forward(half, n, carry):
-        cosine = trig[pl.ds(n, 1), :]
-        sine = trig[pl.ds(STEPS + n, 1), :]
+    def forward(half, n):
+        cosine = trig[n : n + 1, :]
+        sine = trig[STEPS + n : STEPS + n + 1, :]
         for b in range(blocks):
             at = span(b)
             spread = across(statics[DEPTH, half, at, :] * east[n, half, at, :])
@@ -240,7 +244,7 @@
                 height[half, at, :] - (spread + along(flux, half, b))
             )
             height[half, at, :] = new
-            press[half, inner(b), :] = (0.5 * PRESS_RATE) * new + (
+            press[half, inner(b), :] = new + (
                 cosine * statics[COS, half, at, :] + sine * statics[SIN, half, at, :]
             )
         for b in range(blocks):
@@ -255,7 +259,6 @@
             )
             north[n + 1, half, at, :] = north_new
             flux[half, inner(b), :] = statics[DEPTH, half, at, :] * north_new
-        return carry
 
     shared = []
     for side in range(2):
@@ -273,55 +276,69 @@
             )
             shared[-1].start()
 
-    lax.fori_loop(0, STEPS, functools.partial(forward, 0), 0)
+    for n in range(STEPS):
+        forward(0, n)
+
+    for copy in shared:
+        copy.wait_recv()
+
+    def unpack(ref, at, f, own):
+        rims = turned(jnp.where(slot == f, ref[0, at, :], ref[1, at, :]), -f)
+        return jnp.where(slot < 2, rims, own_edges(own))
+
+    for b in range(blocks):
+        at = span(b)
+        fields = [unpack(arrived, at, f, statics[f + 1, 0, at, :]) for f in range(4)]
+        statics[SEA, 1, at, :] = jnp.where(fields[0] > 0.0, 1.0, 0.0)
+        for f in range(4):
+            statics[f + 1, 1, at, :] = fields[f]
+
+    def state_place(f, b):
+        if b < blocks - 1:
+            return pl.ds(b * BLOCK, BLOCK), f
+        return pl.ds(f * BLOCK, BLOCK), 3
 
     for halo in halos:
         halo.wait_recv()
-    relays = [
-        pltpu.make_async_remote_copy(
-            src_ref=arrived.at[side, pl.ds(rows, rows - BLOCK)],
-            dst_ref=next_rim.at[side],
-            send_sem=rim_send.at[side],
-            recv_sem=rim_recv.at[side],
-            device_id=(back, cell),
-            device_id_type=MESH,
-        )
-        for side in range(2)
-    ]
-    for relay in relays:
-        relay.start()
-
-    for copy in shared:
-        copy.wait_recv()
-
-    def unpack(ref, at, f, own):
-        rims = turned(
-            jnp.where(slot == f, ref[0, at, :], ref[1, at, :]),
-            -f,
-        )
-        return jnp.where(slot < 2, rims, own_edges(own))
-
-    def unpack_state(ref, offset, f, b, own):
-        if b < blocks - 1:
-            return unpack(ref, pl.ds(offset + b * BLOCK, BLOCK), f, own)
-        return unpack(ref, pl.ds(offset + f * BLOCK, BLOCK), 3, own)
-
-    for b in range(blocks):
-        at = span(b)
-        fields = [unpack(arrived, at, f, statics[f + 1, 0, at, :]) for f in range(4)]
-        sea = jnp.where(fields[0] > 0.0, 1.0, 0.0)
-        statics[SEA, 1, at, :] = sea
-        for f in range(4):
-            statics[f + 1, 1, at, :] = fields[f]
-        state = [sea * unpack_state(arrived, rows, f, b, start[f, at, :]) for f in range(3)]
-        height[1, at, :] = state[0]
-        east[0, 1, at, :] = state[1]
-        north[0, 1, at, :] = state[2]
-        flux[1, inner(b), :] = fields[1] * state[2]
-
-    lax.fori_loop(0, STEPS, functools.partial(forward, 1), 0)
-
     lost = 2 * STEPS
+    near_slots = []
+    for f in range(3):
+        offset = lax.rem(lane + (4 - f) * RIM, LANES)
+        near_slots.append((offset < lost) | ((offset >= 2 * RIM - lost) & (offset < 2 * RIM)))
+    edge_start = {}
+    for b in range(blocks):
+        for f in range(3):
+            at, slot_at = state_place(f, b)
+            edge_start[f, b] = unpack(
+                arrived.at[:, state_rows], at, slot_at, start[f, span(b), :]
+            )
+    for b in range(blocks - 1):
+        mixed = turned(edge_start[b, blocks - 1], 3)
+        for f in range(3):
+            mixed = jnp.where(near_slots[f], turned(edge_start[f, b], f), mixed)
+        own_rim[span(b), :] = mixed
+    relay = pltpu.make_async_remote_copy(
+        src_ref=own_rim,
+        dst_ref=next_rim,
+        send_sem=rim_send,
+        recv_sem=rim_recv,
+        device_id=(back, cell),
+        device_id_type=MESH,
+    )
+    relay.start()
+    for b in range(blocks):
+        at = span(b)
+        sea = statics[SEA, 1, at, :]
+        speed = (1.0 / SCALE) * sea
+        height[1, at, :] = sea * edge_start[0, b]
+        east[0, 1, at, :] = speed * edge_start[1, b]
+        north_now = speed * edge_start[2, b]
+        north[0, 1, at, :] = north_now
+        flux[1, inner(b), :] = statics[DEPTH, 1, at, :] * north_now
+
+    for n in range(STEPS):
+        forward(1, n)
+
     outer = (lane < lost) | (lane >= LANES - lost)
 
     def whole(body, edges):
@@ -337,7 +354,7 @@
         sea = statics[SEA, 0, at, :]
         for f in range(3):
             ends = [
-                height[half, at, :] if f == 0 else (east, north)[f - 1][STEPS, half, at, :]
+                height[half, at, :] if f == 0 else SCALE * (east, north)[f - 1][STEPS, half, at, :]
                 for half in range(2)
             ]
             defect[f, at, :] = sea * (whole(*ends) - next_start[f, at, :])
@@ -353,18 +370,24 @@
     defect_store = pltpu.make_async_copy(defect, defect_out.at[0], out_sem.at[0])
     defect_store.start()
 
-    for relay in relays:
-        relay.wait_recv()
+    relay.wait_recv()
     for b in range(blocks):
         at = span(b)
         for half in range(2):
-            keep = statics[KEEP, half, at, :]
+            keep = SCALE * statics[KEEP, half, at, :]
             misses = []
             for f in range(3):
                 miss = defect[f, at, :]
                 if half == 1:
-                    end = height[1, at, :] if f == 0 else (east, north)[f - 1][STEPS, 1, at, :]
-                    target = unpack_state(next_rim, 0, f, b, next_start[f, at, :])
+                    end = height[1, at, :]
+                    if f > 0:
+                        end = SCALE * (east, north)[f - 1][STEPS, 1, at, :]
+                    place, slot_at = state_place(f, b)
+                    target = jnp.where(
+                        slot < 2,
+                        turned(next_rim[place, :], -slot_at),
+                        own_edges(next_start[f, at, :]),
+                    )
                     miss = edges_from(miss, statics[SEA, 1, at, :] * (end - target))
                 misses.append(miss)
             east_part = keep * misses[1]
@@ -380,7 +403,7 @@
         for b in range(blocks):
             at = span(b)
             slope = across(adjoint_east[half, at, :]) + along(flux, half, b)
-            new = statics[SEA, half, at, :] * (height[half, at, :] + (0.5 * PRESS_RATE) * slope)
+            new = statics[SEA, half, at, :] * (height[half, at, :] + slope)
             height[half, at, :] = new
             press[half, inner(b), :] = new
 
@@ -396,8 +419,7 @@
             north_part + turn * east_part + depth * along(press, half, b),
         )
 
-    def adjoint(i, carry):
-        n = STEPS - 1 - i
+    def adjoint(n):
         for half in range(2):
             adjoint_height(half)
         for half in range(2):
@@ -412,9 +434,9 @@
                 total[half, at, :] = total[half, at, :] + (
                     east_new * east[n, half, at, :] + north_new * north[n, half, at, :]
                 )
-        return carry
-
-    lax.fori_loop(0, STEPS - 1, adjoint, 0)
+
+    for n in range(STEPS - 1, 0, -1):
+        adjoint(n)
 
     for b in range(blocks):
         at = span(b)
@@ -443,7 +465,7 @@
     behind_copy.wait_recv()
     for b in range(blocks):
         at = span(b)
-        sea = statics[SEA, 0, at, :]
+        sea = (1.0 / SCALE) * statics[SEA, 0, at, :]
         body = adjoint_flow(0, b)
         edges = adjoint_flow(1, b)
         grad[0, at, :] = whole(height[0, at, :], height[1, at, :]) - behind[0, at, :]
@@ -456,15 +478,12 @@
     for step in range(1, slices):
         share_copies[step - 1].wait_recv()
         summed = summed + share_in[step]
-    share_out[...] = summed * (-1.0 / slices)
-    drag_store = pltpu.make_async_copy(share_out, drag_out, out_sem.at[2])
-    drag_store.start()
-
-    for copy in pieces + shared + halos + [start_copy] + relays + [behind_copy] + share_copies:
+    drag_out[...] = summed * (-1.0 / slices)
+
+    for copy in pieces + shared + halos + [start_copy, relay, behind_copy] + share_copies:
         copy.wait_send()
     defect_store.wait()
     grad_store.wait()
-    drag_store.wait()
 
 
 def handed_over(*refs):
@@ -494,7 +513,7 @@
         functools.partial(kernel, slices, cells),
         out_shape=(f32(*start_states.shape), f32(*start_states.shape), f32(share, lanes)),
         in_specs=[hbm] * 7,
-        out_specs=(left,) * 3,
+        out_specs=(left, left, pl.BlockSpec(memory_space=pltpu.VMEM)),
         scratch_shapes=[
             f32(3, rows, lanes),
             pltpu.VMEM((rows, lanes), jnp.int32),
@@ -513,7 +532,8 @@
             f32(2, wide, lanes),
             f32(2, rows + rim_rows, lanes),
             f32(2, rows + rim_rows, lanes),
-            f32(2, rim_rows, lanes),
+            f32(rim_rows, lanes),
+            f32(rim_rows, lanes),
             f32(3, rows, lanes),
             f32(3, rows, lanes),
             f32(3, rows, lanes),
@@ -521,17 +541,16 @@
             f32(2, rows, lanes),
             f32(slices, share, lanes),
             f32(slices, share, lanes),
-            f32(share, lanes),
             sems((7,)),
-            sems((3,)),
+            sems((2,)),
             sems((2, math.gcd(slices, 8))),
             sems((2, math.gcd(slices, 8))),
             sems((2,)),
             sems((2,)),
             sems,
             sems,
-            sems((2,)),
-            sems((2,)),
+            sems,
+            sems,
             sems,
             sems,
             sems((slices,)),

time: 22.3 us -> 22.3 us (level)
  no operation moved by 1% of the time
where the time goes in v4:
time: 22.3 us; the launch traced here: 22.2 us
  Pallas kernels  21.6 us (97%)
  between operations  0.64 us (3%)
    pallas_call x1, Pallas kernels, local(): pl.pallas_call(functools.partial(kernel, slices, cells), out_shape=(f32(*...  20.8 us
    pallas_call x1, Pallas kernels, local(): pl.pallas_call(handed_over, out_shape=tuple((jax.ShapeDtypeStruct(r.shape...  0.77 us

profile of v4, /device:TPU:0, one launch (start us, length us, event | category | flops | bytes accessed | tf_op | source)
XLA Modules:
  0.0 22.2 jit_solution(9705440325806041375)
XLA Ops:
  0.6 20.8 %shard_map.94 = (f32[1,3,128,128]{3,2,1,0:T(8,128)S(1)}, f32[1,3,128,128]{3,2,1,0:T(8,128)S(1)}, f32[16,128]{1,0:T(8,128)S(1)}) custom-call(f32[1,3,128,128]{3,2,1,0:T(8,128)} %start_ref.1, s32[128,128]{1,0:T(8,128)} %mask_ref.1, s32[128,128]{1,0:T(8,128)} %class_ref.1, f32[8]{0:T(128)} %depths_ref.1, f32[128,128]{1,0:T(8,128)} %drag_ref.1, ...), custom_call_target="tpu_custom_call" | custom-call | tf_op jit(solution)/shard_map/pallas_call | solution.py:512
  21.4 0.8 %shard_map.95 = (f32[1,3,128,128]{3,2,1,0:T(8,128)}, f32[1,3,128,128]{3,2,1,0:T(8,128)}, f32[16,128]{1,0:T(8,128)}) custom-call(f32[1,3,128,128]{3,2,1,0:T(8,128)S(1)} %get-tuple-element.6.refs_0_, f32[1,3,128,128]{3,2,1,0:T(8,128)S(1)} %get-tuple-element.7.refs_1_, f32[16,128]{1,0:T(8,128)S(1)} %get-tuple-element.8.refs_2_), custom_call_target="tpu_custom_call" | custom-call | tf_op jit(solution)/shard_map/pallas_call | solution.py:565

commit v5 on v4

--- a/solution.py
+++ b/solution.py
@@ -3,6 +3,7 @@
 
 import jax
 import jax.numpy as jnp
+import numpy as np
 from jax import lax
 from jax.experimental import pallas as pl
 from jax.experimental.pallas import tpu as pltpu
@@ -34,6 +35,7 @@
     drag_ref,
     cos_ref,
     sin_ref,
+    rotation_ref,
     defect_out,
     grad_out,
     drag_out,
@@ -104,6 +106,7 @@
                 (drag_ref, drag),
                 (cos_ref, tides.at[0]),
                 (sin_ref, tides.at[1]),
+                (rotation_ref, rotation),
                 (start_ref.at[0], start),
             )
         )
@@ -209,56 +212,6 @@
         device_id=(back, cell),
         device_id_type=MESH,
     )
-    start_copy.start()
-
-    latitude = lax.broadcasted_iota(jnp.int32, (rows, LANES), 0).astype(jnp.float32)
-    latitude = math.pi * ((latitude + 0.5) / rows - 0.5)
-    rotation[...] = ROTATION_RATE * jnp.sin(latitude)
-    unit = 2.0 * math.pi / (slices * STEPS)
-    number = lax.broadcasted_iota(jnp.int32, (STEPS, LANES), 0) + me * STEPS
-    phase = number.astype(jnp.float32) * unit
-    trig[0:STEPS, :] = jnp.cos(phase)
-    trig[STEPS : 2 * STEPS, :] = jnp.sin(phase)
-    blank = jnp.zeros((PAD, LANES), jnp.float32)
-    for ref in (flux, press):
-        for half in range(2):
-            ref[half, 0:PAD, :] = blank
-            ref[half, PAD + rows : 2 * PAD + rows, :] = blank
-    for b in range(blocks):
-        at = span(b)
-        sea = statics[SEA, 0, at, :]
-        height[0, at, :] = sea * start[0, at, :]
-        speed = (1.0 / SCALE) * sea
-        east[0, 0, at, :] = speed * start[1, at, :]
-        north_now = speed * start[2, at, :]
-        north[0, 0, at, :] = north_now
-        flux[0, inner(b), :] = statics[DEPTH, 0, at, :] * north_now
-
-    def forward(half, n):
-        cosine = trig[n : n + 1, :]
-        sine = trig[STEPS + n : STEPS + n + 1, :]
-        for b in range(blocks):
-            at = span(b)
-            spread = across(statics[DEPTH, half, at, :] * east[n, half, at, :])
-            new = statics[SEA, half, at, :] * (
-                height[half, at, :] - (spread + along(flux, half, b))
-            )
-            height[half, at, :] = new
-            press[half, inner(b), :] = new + (
-                cosine * statics[COS, half, at, :] + sine * statics[SIN, half, at, :]
-            )
-        for b in range(blocks):
-            at = span(b)
-            turn = rotation[at, :]
-            east_now = east[n, half, at, :]
-            north_now = north[n, half, at, :]
-            keep = statics[KEEP, half, at, :]
-            north_new = keep * (north_now - along(press, half, b) - turn * east_now)
-            east[n + 1, half, at, :] = keep * (
-                east_now - across(press[half, inner(b), :]) + turn * north_now
-            )
-            north[n + 1, half, at, :] = north_new
-            flux[half, inner(b), :] = statics[DEPTH, half, at, :] * north_new
 
     shared = []
     for side in range(2):
@@ -275,6 +228,53 @@
                 )
             )
             shared[-1].start()
+    start_copy.start()
+
+    unit = 2.0 * math.pi / (slices * STEPS)
+    number = lax.broadcasted_iota(jnp.int32, (STEPS, LANES), 0) + me * STEPS
+    phase = number.astype(jnp.float32) * unit
+    trig[0:STEPS, :] = jnp.cos(phase)
+    trig[STEPS : 2 * STEPS, :] = jnp.sin(phase)
+    blank = jnp.zeros((PAD, LANES), jnp.float32)
+    for ref in (flux, press):
+        for half in range(2):
+            ref[half, 0:PAD, :] = blank
+            ref[half, PAD + rows : 2 * PAD + rows, :] = blank
+    for b in range(blocks):
+        at = span(b)
+        sea = statics[SEA, 0, at, :]
+        height[0, at, :] = sea * start[0, at, :]
+        speed = (1.0 / SCALE) * sea
+        east[0, 0, at, :] = speed * start[1, at, :]
+        north_now = speed * start[2, at, :]
+        north[0, 0, at, :] = north_now
+        flux[0, inner(b), :] = statics[DEPTH, 0, at, :] * north_now
+
+    def forward(half, n):
+        cosine = trig[n : n + 1, :]
+        sine = trig[STEPS + n : STEPS + n + 1, :]
+        for b in range(blocks):
+            at = span(b)
+            spread = across(statics[DEPTH, half, at, :] * east[n, half, at, :])
+            new = statics[SEA, half, at, :] * (
+                height[half, at, :] - (spread + along(flux, half, b))
+            )
+            height[half, at, :] = new
+            press[half, inner(b), :] = new + (
+                cosine * statics[COS, half, at, :] + sine * statics[SIN, half, at, :]
+            )
+        for b in range(blocks):
+            at = span(b)
+            turn = rotation[at, :]
+            east_now = east[n, half, at, :]
+            north_now = north[n, half, at, :]
+            keep = statics[KEEP, half, at, :]
+            north_new = keep * (north_now - along(press, half, b) - turn * east_now)
+            east[n + 1, half, at, :] = keep * (
+                east_now - across(press[half, inner(b), :]) + turn * north_now
+            )
+            north[n + 1, half, at, :] = north_new
+            flux[half, inner(b), :] = statics[DEPTH, half, at, :] * north_new
 
     for n in range(STEPS):
         forward(0, n)
@@ -509,10 +509,13 @@
     left = pl.BlockSpec(memory_space=pl.ANY)
     wide = rows + 2 * PAD
     rim_rows = rows - BLOCK
+    latitude = np.pi * ((np.arange(rows) + 0.5) / rows - 0.5)
+    turning = np.broadcast_to((ROTATION_RATE * np.sin(latitude))[:, None], (rows, lanes))
+    turning = jnp.asarray(np.ascontiguousarray(turning, dtype=np.float32))
     results = pl.pallas_call(
         functools.partial(kernel, slices, cells),
         out_shape=(f32(*start_states.shape), f32(*start_states.shape), f32(share, lanes)),
-        in_specs=[hbm] * 7,
+        in_specs=[hbm] * 8,
         out_specs=(left, left, pl.BlockSpec(memory_space=pltpu.VMEM)),
         scratch_shapes=[
             f32(3, rows, lanes),
@@ -541,7 +544,7 @@
             f32(2, rows, lanes),
             f32(slices, share, lanes),
             f32(slices, share, lanes),
-            sems((7,)),
+            sems((8,)),
             sems((2,)),
             sems((2, math.gcd(slices, 8))),
             sems((2, math.gcd(slices, 8))),
@@ -560,7 +563,7 @@
             collective_id=0, has_side_effects=True, vmem_limit_bytes=32 * 1024 * 1024
         ),
     )(
-        *(pltpu.with_memory_space_constraint(x, pltpu.HBM) for x in operands),
+        *(pltpu.with_memory_space_constraint(x, pltpu.HBM) for x in (*operands, turning)),
     )
     return pl.pallas_call(
         handed_over,

time: 22.3 us -> 22.4 us (level)
  no operation moved by 1% of the time
where the time goes in v5:
time: 22.4 us; the launch traced here: 22.2 us
  Pallas kernels  21.6 us (96%)
  between operations  0.64 us (3%)
    pallas_call x1, Pallas kernels, local(): pl.pallas_call(functools.partial(kernel, slices, cells), out_shape=(f32(*...  20.8 us
    pallas_call x1, Pallas kernels, local(): pl.pallas_call(handed_over, out_shape=tuple((jax.ShapeDtypeStruct(r.shape...  0.77 us

profile of v5, /device:TPU:0, one launch (start us, length us, event | category | flops | bytes accessed | tf_op | source)
XLA Modules:
  0.0 22.2 jit_solution(9827559758706998713)
XLA Ops:
  0.6 20.8 %shard_map.103 = (f32[1,3,128,128]{3,2,1,0:T(8,128)S(1)}, f32[1,3,128,128]{3,2,1,0:T(8,128)S(1)}, f32[16,128]{1,0:T(8,128)S(1)}) custom-call(f32[1,3,128,128]{3,2,1,0:T(8,128)} %start_ref.1, s32[128,128]{1,0:T(8,128)} %mask_ref.1, s32[128,128]{1,0:T(8,128)} %class_ref.1, f32[8]{0:T(128)} %depths_ref.1, f32[128,128]{1,0:T(8,128)} %drag_ref.1, ...), custom_call_target="tpu_custom_call" | custom-call | tf_op jit(solution)/shard_map/pallas_call | solution.py:515
  21.5 0.8 %shard_map.104 = (f32[1,3,128,128]{3,2,1,0:T(8,128)}, f32[1,3,128,128]{3,2,1,0:T(8,128)}, f32[16,128]{1,0:T(8,128)}) custom-call(f32[1,3,128,128]{3,2,1,0:T(8,128)S(1)} %get-tuple-element.6.refs_0_, f32[1,3,128,128]{3,2,1,0:T(8,128)S(1)} %get-tuple-element.7.refs_1_, f32[16,128]{1,0:T(8,128)S(1)} %get-tuple-element.8.refs_2_), custom_call_target="tpu_custom_call" | custom-call | tf_op jit(solution)/shard_map/pallas_call | solution.py:568

commit v6 on v5

--- a/solution.py
+++ b/solution.py
@@ -174,7 +174,7 @@
         packed[1, at, :] = east_side
     pl.semaphore_wait(barrier, slices + 1)
 
-    group = math.gcd(slices, 8)
+    group = math.gcd(slices, 2)
     piece = rows // group
     rank = lax.rem(me, group)
     piece_rows = pl.ds(pl.multiple_of(rank * piece, piece), piece)
@@ -546,8 +546,8 @@
             f32(slices, share, lanes),
             sems((8,)),
             sems((2,)),
-            sems((2, math.gcd(slices, 8))),
-            sems((2, math.gcd(slices, 8))),
+            sems((2, math.gcd(slices, 2))),
+            sems((2, math.gcd(slices, 2))),
             sems((2,)),
             sems((2,)),
             sems,

time: 22.4 us -> 22.9 us (1.022)
  Pallas kernels: 21.6 us -> 22.1 us
    pallas_call x1, Pallas kernels: 20.8 us -> 21.3 us  [local(): pl.pallas_call(functools.partial(kernel, slices, cells), out_shape=(f32(*...]
where the time goes in v6:
time: 22.9 us; the launch traced here: 22.7 us
  Pallas kernels  22.1 us (97%)
  between operations  0.64 us (3%)
    pallas_call x1, Pallas kernels, local(): pl.pallas_call(functools.partial(kernel, slices, cells), out_shape=(f32(*...  21.3 us
    pallas_call x1, Pallas kernels, local(): pl.pallas_call(handed_over, out_shape=tuple((jax.ShapeDtypeStruct(r.shape...  0.77 us

profile of v6, /device:TPU:0, one launch (start us, length us, event | category | flops | bytes accessed | tf_op | source)
XLA Modules:
  0.0 22.7 jit_solution(4044001060811509542)
XLA Ops:
  0.6 21.3 %shard_map.103 = (f32[1,3,128,128]{3,2,1,0:T(8,128)S(1)}, f32[1,3,128,128]{3,2,1,0:T(8,128)S(1)}, f32[16,128]{1,0:T(8,128)S(1)}) custom-call(f32[1,3,128,128]{3,2,1,0:T(8,128)} %start_ref.1, s32[128,128]{1,0:T(8,128)} %mask_ref.1, s32[128,128]{1,0:T(8,128)} %class_ref.1, f32[8]{0:T(128)} %depths_ref.1, f32[128,128]{1,0:T(8,128)} %drag_ref.1, ...), custom_call_target="tpu_custom_call" | custom-call | tf_op jit(solution)/shard_map/pallas_call | solution.py:515
  21.9 0.8 %shard_map.104 = (f32[1,3,128,128]{3,2,1,0:T(8,128)}, f32[1,3,128,128]{3,2,1,0:T(8,128)}, f32[16,128]{1,0:T(8,128)}) custom-call(f32[1,3,128,128]{3,2,1,0:T(8,128)S(1)} %get-tuple-element.6.refs_0_, f32[1,3,128,128]{3,2,1,0:T(8,128)S(1)} %get-tuple-element.7.refs_1_, f32[16,128]{1,0:T(8,128)S(1)} %get-tuple-element.8.refs_2_), custom_call_target="tpu_custom_call" | custom-call | tf_op jit(solution)/shard_map/pallas_call | solution.py:568

commit v7 on v5

--- a/solution.py
+++ b/solution.py
@@ -135,6 +135,8 @@
         return value if by % 4 == 0 else pltpu.roll(value, by % 4 * RIM, 1)
 
     def pack(parts):
+        lane = lax.broadcasted_iota(jnp.int32, parts[0].shape, 1)
+        slot = lane // RIM
         west = parts[0]
         east_side = turned(parts[0], 2)
         for f in range(1, 4):
@@ -145,40 +147,26 @@
     def own_edges(value):
         return jnp.where(slot == 3, value, turned(value, 2))
 
-    loads[-1].wait()
-    for b in range(blocks - 1):
-        parts = [start[f, span(b), :] for f in range(3)]
-        parts.append(start[b, span(blocks - 1), :])
-        west, east_side = pack(parts)
-        packed[0, pl.ds(rows + b * BLOCK, BLOCK), :] = west
-        packed[1, pl.ds(rows + b * BLOCK, BLOCK), :] = east_side
-
-    for load in loads[:-1]:
-        load.wait()
-    for b in range(blocks):
-        at = span(b)
+    def worked_out(at):
         sea = mask[at, :].astype(jnp.float32)
-        depth = jnp.zeros((BLOCK, LANES), jnp.float32)
         kind = classes[at, :]
+        depth = jnp.zeros(kind.shape, jnp.float32)
         for c in range(table.shape[0]):
             depth = jnp.where(kind == c, table[c], depth)
+        keep = sea / (1.0 + drag[at, :])
         depth = (0.5 * FLUX_RATE * SCALE) * depth
-        keep = sea / (1.0 + drag[at, :])
-        cosine = tides[0, at, :]
-        sine = tides[1, at, :]
-        fields = (sea, keep, depth, cosine, sine)
-        for f in range(5):
-            statics[f, 0, at, :] = fields[f]
-        west, east_side = pack(fields[1:])
-        packed[0, at, :] = west
-        packed[1, at, :] = east_side
-    pl.semaphore_wait(barrier, slices + 1)
+        return sea, keep, depth, tides[0, at, :], tides[1, at, :]
 
     group = math.gcd(slices, 8)
     piece = rows // group
     rank = lax.rem(me, group)
     piece_rows = pl.ds(pl.multiple_of(rank * piece, piece), piece)
     sides = ((0, west_cell), (1, east_cell))
+    for load in loads[:-1]:
+        load.wait()
+    packed[0, piece_rows, :], packed[1, piece_rows, :] = pack(worked_out(piece_rows)[1:])
+    pl.semaphore_wait(barrier, slices + 1)
+
     pieces = [
         pltpu.make_async_remote_copy(
             src_ref=packed.at[side, piece_rows],
@@ -190,6 +178,17 @@
         )
         for side, other in sides
     ]
+    for copy in pieces:
+        copy.start()
+
+    loads[-1].wait()
+    for b in range(blocks - 1):
+        parts = [start[f, span(b), :] for f in range(3)]
+        parts.append(start[b, span(blocks - 1), :])
+        west, east_side = pack(parts)
+        packed[0, pl.ds(rows + b * BLOCK, BLOCK), :] = west
+        packed[1, pl.ds(rows + b * BLOCK, BLOCK), :] = east_side
+
     state_rows = pl.ds(rows, rows - BLOCK)
     halos = [
         pltpu.make_async_remote_copy(
@@ -202,8 +201,13 @@
         )
         for side, other in sides
     ]
-    for copy in pieces + halos:
-        copy.start()
+    for halo in halos:
+        halo.start()
+    for b in range(blocks):
+        fields = worked_out(span(b))
+        for f in range(5):
+            statics[f, 0, span(b), :] = fields[f]
+
     start_copy = pltpu.make_async_remote_copy(
         src_ref=start,
         dst_ref=next_start,
@@ -250,9 +254,9 @@
         north[0, 0, at, :] = north_now
         flux[0, inner(b), :] = statics[DEPTH, 0, at, :] * north_now
 
-    def forward(half, n):
-        cosine = trig[n : n + 1, :]
-        sine = trig[STEPS + n : STEPS + n + 1, :]
+    def forward(half, n, carry):
+        cosine = trig[pl.ds(n, 1), :]
+        sine = trig[pl.ds(STEPS + n, 1), :]
         for b in range(blocks):
             at = span(b)
             spread = across(statics[DEPTH, half, at, :] * east[n, half, at, :])
@@ -263,6 +267,7 @@
             press[half, inner(b), :] = new + (
                 cosine * statics[COS, half, at, :] + sine * statics[SIN, half, at, :]
             )
+        results = []
         for b in range(blocks):
             at = span(b)
             turn = rotation[at, :]
@@ -270,14 +275,14 @@
             north_now = north[n, half, at, :]
             keep = statics[KEEP, half, at, :]
             north_new = keep * (north_now - along(press, half, b) - turn * east_now)
-            east[n + 1, half, at, :] = keep * (
-                east_now - across(press[half, inner(b), :]) + turn * north_now
-            )
-            north[n + 1, half, at, :] = north_new
-            flux[half, inner(b), :] = statics[DEPTH, half, at, :] * north_new
-
-    for n in range(STEPS):
-        forward(0, n)
+            east_new = keep * (east_now - across(press[half, inner(b), :]) + turn * north_now)
+            results.append((east_new, north_new, statics[DEPTH, half, at, :] * north_new))
+        for b in range(blocks):
+            at = span(b)
+            east[n + 1, half, at, :], north[n + 1, half, at, :], flux[half, inner(b), :] = results[b]
+        return carry
+
+    lax.fori_loop(0, STEPS, functools.partial(forward, 0), 0)
 
     for copy in shared:
         copy.wait_recv()
@@ -336,8 +341,7 @@
         north[0, 1, at, :] = north_now
         flux[1, inner(b), :] = statics[DEPTH, 1, at, :] * north_now
 
-    for n in range(STEPS):
-        forward(1, n)
+    lax.fori_loop(0, STEPS, functools.partial(forward, 1), 0)
 
     outer = (lane < lost) | (lane >= LANES - lost)
 
@@ -419,7 +423,8 @@
             north_part + turn * east_part + depth * along(press, half, b),
         )
 
-    def adjoint(n):
+    def adjoint(i, carry):
+        n = STEPS - 1 - i
         for half in range(2):
             adjoint_height(half)
         for half in range(2):
@@ -435,8 +440,9 @@
                     east_new * east[n, half, at, :] + north_new * north[n, half, at, :]
                 )
 
-    for n in range(STEPS - 1, 0, -1):
-        adjoint(n)
+        return carry
+
+    lax.fori_loop(0, STEPS - 1, adjoint, 0)
 
     for b in range(blocks):
         at = span(b)

time: 22.4 us -> 22.7 us (1.013)
  Pallas kernels: 21.6 us -> 21.9 us
    pallas_call x1, Pallas kernels: 20.8 us -> 21.2 us  [local(): pl.pallas_call(functools.partial(kernel, slices, cells), out_shape=(f32(*...]
where the time goes in v7:
time: 22.7 us; the launch traced here: 22.6 us
  Pallas kernels  21.9 us (96%)
  between operations  0.64 us (3%)
    pallas_call x1, Pallas kernels, local(): pl.pallas_call(functools.partial(kernel, slices, cells), out_shape=(f32(*...  21.2 us
    pallas_call x1, Pallas kernels, local(): pl.pallas_call(handed_over, out_shape=tuple((jax.ShapeDtypeStruct(r.shape...  0.77 us

profile of v7, /device:TPU:0, one launch (start us, length us, event | category | flops | bytes accessed | tf_op | source)
XLA Modules:
  0.0 22.6 jit_solution(13254584700546409151)
XLA Ops:
  0.6 21.2 %shard_map.103 = (f32[1,3,128,128]{3,2,1,0:T(8,128)S(1)}, f32[1,3,128,128]{3,2,1,0:T(8,128)S(1)}, f32[16,128]{1,0:T(8,128)S(1)}) custom-call(f32[1,3,128,128]{3,2,1,0:T(8,128)} %start_ref.1, s32[128,128]{1,0:T(8,128)} %mask_ref.1, s32[128,128]{1,0:T(8,128)} %class_ref.1, f32[8]{0:T(128)} %depths_ref.1, f32[128,128]{1,0:T(8,128)} %drag_ref.1, ...), custom_call_target="tpu_custom_call" | custom-call | tf_op jit(solution)/shard_map/pallas_call | solution.py:521
  21.8 0.8 %shard_map.104 = (f32[1,3,128,128]{3,2,1,0:T(8,128)}, f32[1,3,128,128]{3,2,1,0:T(8,128)}, f32[16,128]{1,0:T(8,128)}) custom-call(f32[1,3,128,128]{3,2,1,0:T(8,128)S(1)} %get-tuple-element.6.refs_0_, f32[1,3,128,128]{3,2,1,0:T(8,128)S(1)} %get-tuple-element.7.refs_1_, f32[16,128]{1,0:T(8,128)S(1)} %get-tuple-element.8.refs_2_), custom_call_target="tpu_custom_call" | custom-call | tf_op jit(solution)/shard_map/pallas_call | solution.py:574

commit v8 on v7

--- a/solution.py
+++ b/solution.py
@@ -254,9 +254,9 @@
         north[0, 0, at, :] = north_now
         flux[0, inner(b), :] = statics[DEPTH, 0, at, :] * north_now
 
-    def forward(half, n, carry):
-        cosine = trig[pl.ds(n, 1), :]
-        sine = trig[pl.ds(STEPS + n, 1), :]
+    def forward(half, n):
+        cosine = trig[n : n + 1, :]
+        sine = trig[STEPS + n : STEPS + n + 1, :]
         for b in range(blocks):
             at = span(b)
             spread = across(statics[DEPTH, half, at, :] * east[n, half, at, :])
@@ -267,7 +267,6 @@
             press[half, inner(b), :] = new + (
                 cosine * statics[COS, half, at, :] + sine * statics[SIN, half, at, :]
             )
-        results = []
         for b in range(blocks):
             at = span(b)
             turn = rotation[at, :]
@@ -275,14 +274,14 @@
             north_now = north[n, half, at, :]
             keep = statics[KEEP, half, at, :]
             north_new = keep * (north_now - along(press, half, b) - turn * east_now)
-            east_new = keep * (east_now - across(press[half, inner(b), :]) + turn * north_now)
-            results.append((east_new, north_new, statics[DEPTH, half, at, :] * north_new))
-        for b in range(blocks):
-            at = span(b)
-            east[n + 1, half, at, :], north[n + 1, half, at, :], flux[half, inner(b), :] = results[b]
-        return carry
-
-    lax.fori_loop(0, STEPS, functools.partial(forward, 0), 0)
+            east[n + 1, half, at, :] = keep * (
+                east_now - across(press[half, inner(b), :]) + turn * north_now
+            )
+            north[n + 1, half, at, :] = north_new
+            flux[half, inner(b), :] = statics[DEPTH, half, at, :] * north_new
+
+    for n in range(STEPS):
+        forward(0, n)
 
     for copy in shared:
         copy.wait_recv()
@@ -341,7 +340,8 @@
         north[0, 1, at, :] = north_now
         flux[1, inner(b), :] = statics[DEPTH, 1, at, :] * north_now
 
-    lax.fori_loop(0, STEPS, functools.partial(forward, 1), 0)
+    for n in range(STEPS):
+        forward(1, n)
 
     outer = (lane < lost) | (lane >= LANES - lost)
 
@@ -423,8 +423,7 @@
             north_part + turn * east_part + depth * along(press, half, b),
         )
 
-    def adjoint(i, carry):
-        n = STEPS - 1 - i
+    def adjoint(n):
         for half in range(2):
             adjoint_height(half)
         for half in range(2):
@@ -440,9 +439,8 @@
                     east_new * east[n, half, at, :] + north_new * north[n, half, at, :]
                 )
 
-        return carry
-
-    lax.fori_loop(0, STEPS - 1, adjoint, 0)
+    for n in range(STEPS - 1, 0, -1):
+        adjoint(n)
 
     for b in range(blocks):
         at = span(b)

time: 22.7 us -> 22.1 us (0.974)
  Pallas kernels: 21.9 us -> 21.3 us
    pallas_call x1, Pallas kernels: 21.2 us -> 20.5 us  [local(): pl.pallas_call(functools.partial(kernel, slices, cells), out_shape=(f32(*...]
where the time goes in v8:
time: 22.1 us; the launch traced here: 21.9 us
  Pallas kernels  21.3 us (96%)
  between operations  0.64 us (3%)
    pallas_call x1, Pallas kernels, local(): pl.pallas_call(functools.partial(kernel, slices, cells), out_shape=(f32(*...  20.5 us
    pallas_call x1, Pallas kernels, local(): pl.pallas_call(handed_over, out_shape=tuple((jax.ShapeDtypeStruct(r.shape...  0.77 us

profile of v8, /device:TPU:0, one launch (start us, length us, event | category | flops | bytes accessed | tf_op | source)
XLA Modules:
  0.0 21.9 jit_solution(10654755271254136678)
XLA Ops:
  0.6 20.5 %shard_map.103 = (f32[1,3,128,128]{3,2,1,0:T(8,128)S(1)}, f32[1,3,128,128]{3,2,1,0:T(8,128)S(1)}, f32[16,128]{1,0:T(8,128)S(1)}) custom-call(f32[1,3,128,128]{3,2,1,0:T(8,128)} %start_ref.1, s32[128,128]{1,0:T(8,128)} %mask_ref.1, s32[128,128]{1,0:T(8,128)} %class_ref.1, f32[8]{0:T(128)} %depths_ref.1, f32[128,128]{1,0:T(8,128)} %drag_ref.1, ...), custom_call_target="tpu_custom_call" | custom-call | tf_op jit(solution)/shard_map/pallas_call | solution.py:519
  21.1 0.8 %shard_map.104 = (f32[1,3,128,128]{3,2,1,0:T(8,128)}, f32[1,3,128,128]{3,2,1,0:T(8,128)}, f32[16,128]{1,0:T(8,128)}) custom-call(f32[1,3,128,128]{3,2,1,0:T(8,128)S(1)} %get-tuple-element.6.refs_0_, f32[1,3,128,128]{3,2,1,0:T(8,128)S(1)} %get-tuple-element.7.refs_1_, f32[16,128]{1,0:T(8,128)S(1)} %get-tuple-element.8.refs_2_), custom_call_target="tpu_custom_call" | custom-call | tf_op jit(solution)/shard_map/pallas_call | solution.py:572
